TPU v7x, 32 devices: a whole 2x2x4 slice. The times are simulated.
32 devices in a mesh: rep: 4 (over y, x), shard: 8 (over z, core).
Axes of the slice: x: 2, y: 2, z: 4, core: 2. Of those that a mesh axis runs over, the one named last changes fastest.
Arguments:
- tokens: bfloat16 [16384, 1536], P(('rep', 'shard')), may hold values from -6 to 6
- lengths: int32 [32], P(('rep', 'shard')), may hold values from 128 to 512, as said below
- buckets: int32 [1023], replicated, may hold values from 0 to 31, as said below
- w_query: bfloat16 [1536, 768], P('shard'), may hold values from -0.0390625 to 0.0390625
- w_key: bfloat16 [1536, 768], P('shard'), may hold values from -0.15625 to 0.15625
- w_value: bfloat16 [1536, 768], P('shard'), may hold values from -0.15625 to 0.15625
- w_out: bfloat16 [768, 1536], P('shard'), may hold values from -1.25 to 1.25
- w_gate: bfloat16 [1536, 3968], P('shard'), may hold values from -0.15625 to 0.15625
- w_up: bfloat16 [1536, 3968], P('shard'), may hold values from -0.15625 to 0.15625
- w_down: bfloat16 [3968, 1536], P('shard'), may hold values from -0.09375 to 0.09375
- bias_table: bfloat16 [32, 12], P('shard'), may hold values from -4 to 4
- norm_attn: bfloat16 [1536], P('shard'), may hold values from 0.099609375 to 1.8984375
- norm_ffn: bfloat16 [1536], P('shard'), may hold values from 0.099609375 to 1.8984375
- cotangent: bfloat16 [16384, 1536], P(('rep', 'shard')), may hold values from -6 to 6
Outputs:
- output: bfloat16 [16384, 1536], P(('rep', 'shard'))
- grad_tokens: bfloat16 [16384, 1536], P(('rep', 'shard'))
- grad_query: float32 [1536, 768], P('shard')
- grad_key: float32 [1536, 768], P('shard')
- grad_value: float32 [1536, 768], P('shard')
- grad_out: float32 [768, 1536], P('shard')
- grad_gate: float32 [1536, 3968], P('shard')
- grad_up: float32 [1536, 3968], P('shard')
- grad_down: float32 [3968, 1536], P('shard')
- grad_table: float32 [32, 12], P('shard')
- grad_norm_attn: float32 [1536], P('shard')
- grad_norm_ffn: float32 [1536], P('shard')
Inputs may be any that keep to these rules, and one draw needn't show every extreme that they name: `lengths`: some sequence has exactly 512 valid bytes. `buckets`: non-decreasing in the absolute distance on each side; buckets 0 to 15 for distances of 0 or less, 16 to 31 for positive ones.
All inputs are finite; a program needn't handle non-finite values.
Results may differ from a plain program's by a relative error of at most 0.02.
Values may be sent and summed in bfloat16 or wider, within the bound.
No kernel may reach another device: no remote copies, remote signals or barrier semaphores. Data moves between devices by JAX's collectives and lax.ppermute only.
A program may use at most 320 MiB of HBM per device.

v0:
```python
import functools

import jax
import jax.numpy as jnp
from jax import lax
from jax.experimental import pallas as pl
from jax.experimental.pallas import tpu as pltpu
from jax.sharding import PartitionSpec as P

NEG_FILL = -1000000000.0
VMEM_LIMIT = 56 * 1024 * 1024
TOEP = 128
COST_SHARE = 1.0


def cost(flops):
    flops = int(flops * COST_SHARE)
    return pl.CostEstimate(flops=flops, bytes_accessed=flops // 512, transcendentals=0)


def dot_nn(a, b):
    return lax.dot_general(a, b, (((1,), (0,)), ((), ())), preferred_element_type=jnp.float32)


def dot_nt(a, b):
    return lax.dot_general(a, b, (((1,), (1,)), ((), ())), preferred_element_type=jnp.float32)


def dot_tn(a, b):
    return lax.dot_general(a, b, (((0,), (0,)), ((), ())), preferred_element_type=jnp.float32)


def biased_scores(rows_k, rows_q, bias_row, valid, length):
    steps = length // TOEP
    raw = dot_nt(rows_k, rows_q)
    width = bias_row.shape[-1]
    spread = jnp.broadcast_to(bias_row, (TOEP, width))
    table = pltpu.roll(spread, width - (TOEP - 1), 1, stride=1, stride_axis=0)
    blocks = []
    for step in range(steps):
        start = TOEP * (steps - 1 - step)
        row_at = lax.broadcasted_iota(jnp.int32, (TOEP, length), 0) + step * TOEP
        mask = jnp.where(row_at < valid, 0.0, NEG_FILL)
        blocks.append(
            raw[step * TOEP : (step + 1) * TOEP] + table[:, start : start + length] + mask
        )
    return jnp.concatenate(blocks, axis=0)


def attention_forward(valid_ref, bias_ref, q_ref, k_ref, v_ref, ctx_ref, turned_ref, lse_ref, *, head_size):
    length = q_ref.shape[1]
    pair = q_ref.shape[2] // head_size
    q, k, v = q_ref[0], k_ref[0], v_ref[0]
    lane_head = lax.broadcasted_iota(jnp.int32, q.shape, 1) // head_size
    v_turned = v.T
    outs = []
    for head in range(pair):
        own_q = jnp.where(lane_head == head, q, jnp.zeros_like(q))
        scores = biased_scores(k, own_q, bias_ref[0, head : head + 1], valid_ref[0], length)
        top = jnp.max(scores, axis=0, keepdims=True)
        terms = jnp.exp(scores - top)
        total = jnp.sum(terms, axis=0, keepdims=True)
        probs = (terms * (1.0 / total)).astype(jnp.bfloat16)
        lse_ref[0, head : head + 1] = top + jnp.log(total)
        outs.append(dot_nn(v_turned, probs)[head * head_size : (head + 1) * head_size])
    turned = jnp.concatenate(outs, axis=0)
    turned_ref[...] = turned.astype(jnp.bfloat16)
    ctx_ref[...] = turned.T.astype(jnp.bfloat16)


def attention_backward(
    valid_ref, bias_ref, q_ref, k_ref, v_ref, dctx_ref, lse_ref, dq_ref, dk_ref, dv_ref, rel_ref, *, head_size
):
    length = q_ref.shape[1]
    pair = q_ref.shape[2] // head_size
    steps = length // TOEP
    q, k, v, dctx = q_ref[0], k_ref[0], v_ref[0], dctx_ref[...]
    lane_head = lax.broadcasted_iota(jnp.int32, q.shape, 1) // head_size
    k_turned = k.T
    width = bias_ref.shape[-1]
    flip = (
        lax.broadcasted_iota(jnp.int32, (TOEP, TOEP), 0)
        + lax.broadcasted_iota(jnp.int32, (TOEP, TOEP), 1)
        == TOEP - 1
    ).astype(jnp.bfloat16)
    dq_parts = []
    dk = dv = None
    for head in range(pair):
        mine = lane_head == head
        own_q = jnp.where(mine, q, jnp.zeros_like(q))
        own_d = jnp.where(mine, dctx, jnp.zeros_like(dctx))
        scores = biased_scores(k, own_q, bias_ref[0, head : head + 1], valid_ref[0], length)
        probs = jnp.exp(scores - lse_ref[0, head : head + 1])
        d_probs = dot_nt(v, own_d)
        inner = jnp.sum(d_probs * probs, axis=0, keepdims=True)
        d_scores = (probs * (d_probs - inner)).astype(jnp.bfloat16)
        part_v = dot_nn(probs.astype(jnp.bfloat16), own_d)
        part_k = dot_nn(d_scores, own_q)
        dv = part_v if dv is None else dv + part_v
        dk = part_k if dk is None else dk + part_k
        dq_parts.append(dot_nn(k_turned, d_scores)[head * head_size : (head + 1) * head_size])
        fold = None
        for step in range(steps):
            start = TOEP * (steps - 1 - step)
            turned = dot_nn(flip, d_scores[step * TOEP : (step + 1) * TOEP])
            pieces = []
            if start:
                pieces.append(jnp.zeros((TOEP, start), jnp.float32))
            pieces.append(turned)
            if width - start - length:
                pieces.append(jnp.zeros((TOEP, width - start - length), jnp.float32))
            padded = jnp.concatenate(pieces, axis=1)
            fold = padded if fold is None else fold + padded
        lined = pltpu.roll(fold, 0, 1, stride=1, stride_axis=0)
        rel_ref[0, head : head + 1] = jnp.sum(lined, axis=0, keepdims=True)
    dq_ref[0] = jnp.concatenate(dq_parts, axis=0).T.astype(jnp.bfloat16)
    dk_ref[0] = dk.astype(jnp.bfloat16)
    dv_ref[0] = dv.astype(jnp.bfloat16)


def run_forward(valid, bias_rows, qkv, head_size):
    halves, length, wide = qkv.shape
    half = wide // 3
    per = half // 128
    pairs = halves * per
    width = bias_rows.shape[-1]
    spec = lambda kind: pl.BlockSpec((1, length, 128), lambda p: (p // per, 0, kind * per + p % per))
    return pl.pallas_call(
        functools.partial(attention_forward, head_size=head_size),
        grid=(pairs,),
        in_specs=[
            pl.BlockSpec(memory_space=pltpu.SMEM),
            pl.BlockSpec((1, 2, width), lambda p: (p, 0, 0)),
            spec(0), spec(1), spec(2),
        ],
        out_specs=[
            pl.BlockSpec((length, 128), lambda p: (0, p)),
            pl.BlockSpec((128, length), lambda p: (p, 0)),
            pl.BlockSpec((1, 2, length), lambda p: (p, 0, 0)),
        ],
        out_shape=[
            jax.ShapeDtypeStruct((length, halves * half), jnp.bfloat16),
            jax.ShapeDtypeStruct((halves * half, length), jnp.bfloat16),
            jax.ShapeDtypeStruct((pairs, 2, length), jnp.float32),
        ],
        compiler_params=pltpu.CompilerParams(vmem_limit_bytes=VMEM_LIMIT),
        name="attend",
        cost_estimate=cost(8 * pairs * 2 * length * length * 128),
    )(valid, bias_rows, qkv, qkv, qkv)


def run_backward(valid, bias_rows, qkv, d_context, lse, head_size):
    halves, length, wide = qkv.shape
    half = wide // 3
    per = half // 128
    pairs = halves * per
    width = bias_rows.shape[-1]
    spec = lambda kind: pl.BlockSpec((1, length, 128), lambda p: (p // per, 0, kind * per + p % per))
    out_spec = pl.BlockSpec((1, length, 128), lambda p: (p // per, 0, p % per))
    grad = jax.ShapeDtypeStruct((halves, length, half), jnp.bfloat16)
    row = pl.BlockSpec((1, 2, width), lambda p: (p, 0, 0))
    return pl.pallas_call(
        functools.partial(attention_backward, head_size=head_size),
        grid=(pairs,),
        in_specs=[
            pl.BlockSpec(memory_space=pltpu.SMEM),
            row,
            spec(0), spec(1), spec(2),
            pl.BlockSpec((length, 128), lambda p: (0, p)),
            pl.BlockSpec((1, 2, length), lambda p: (p, 0, 0)),
        ],
        out_specs=[out_spec, out_spec, out_spec, row],
        out_shape=[grad, grad, grad, jax.ShapeDtypeStruct((pairs, 2, width), jnp.float32)],
        compiler_params=pltpu.CompilerParams(vmem_limit_bytes=VMEM_LIMIT),
        name="attend_back",
        cost_estimate=cost(16 * pairs * 2 * length * length * 128),
    )(valid, bias_rows, qkv, qkv, qkv, d_context, lse)


EPSILON = 1e-06
AXES = ("team", "wing", "plane", "core")


def split_kernel(at_ref, gate_ref, up_ref, keep_ref, send_ref, *, cuts, piece, padded):
    rows = gate_ref.shape[0]
    first_wing, first_core = at_ref[0] == 0, at_ref[1] == 0
    filler = jnp.zeros((rows, padded - piece), jnp.float32)
    for number, ref in enumerate((gate_ref, up_ref)):
        w = ref[...].astype(jnp.float32)
        for cut in range(cuts):
            sides = []
            for side in (0, 1):
                zero, one = [
                    w[:, (4 * cut + 2 * side + wing) * piece :][:, :piece] for wing in (0, 1)
                ]
                chosen = jnp.where(first_wing, zero, one)
                sides.append(jnp.concatenate([chosen, filler], axis=1).astype(jnp.bfloat16))
            start = (number * cuts + cut) * padded
            to = slice(start, start + padded)
            keep_ref[:, to] = jnp.where(first_core, sides[0], sides[1])
            send_ref[:, to] = jnp.where(first_core, sides[1], sides[0])


def split_columns(at, w_gate, w_up, piece, padded):
    rows, wide = w_gate.shape
    cuts = wide // (4 * piece)
    out = jax.ShapeDtypeStruct((rows, 2 * cuts * padded), jnp.bfloat16)
    whole = pl.BlockSpec(memory_space=pltpu.VMEM)
    return pl.pallas_call(
        functools.partial(split_kernel, cuts=cuts, piece=piece, padded=padded),
        in_specs=[pl.BlockSpec(memory_space=pltpu.SMEM), whole, whole],
        out_specs=[whole, whole],
        out_shape=[out, out],
        compiler_params=pltpu.CompilerParams(vmem_limit_bytes=VMEM_LIMIT),
        name="split",
        cost_estimate=cost(512 * w_gate.size),
    )(at, w_gate, w_up)


def join_kernel(core_ref, mine_ref, other_ref, gate_ref, up_ref, *, cuts, piece, padded):
    rows = gate_ref.shape[0]
    first_core = core_ref[0] == 0
    for number, out_ref in enumerate((gate_ref, up_ref)):
        for cut in range(cuts):
            start = (number * cuts + cut) * padded
            at = slice(start, start + padded)
            for wing in (0, 1):
                of = slice(wing * rows, (wing + 1) * rows)
                mine, other = mine_ref[of, at], other_ref[of, at]
                for side in (0, 1):
                    value = jnp.where(first_core, *((mine, other) if side == 0 else (other, mine)))
                    to = (4 * cut + 2 * side + wing) * piece
                    out_ref[:, to : to + piece] = value.astype(jnp.float32)[:, :piece]


def join_columns(core, mine, other, piece, padded):
    rows = mine.shape[0] // 2
    cuts = mine.shape[1] // (2 * padded)
    out = jax.ShapeDtypeStruct((rows, 4 * cuts * piece), jnp.float32)
    whole = pl.BlockSpec(memory_space=pltpu.VMEM)
    return pl.pallas_call(
        functools.partial(join_kernel, cuts=cuts, piece=piece, padded=padded),
        in_specs=[pl.BlockSpec(memory_space=pltpu.SMEM), whole, whole],
        out_specs=[whole, whole],
        out_shape=[out, out],
        compiler_params=pltpu.CompilerParams(vmem_limit_bytes=VMEM_LIMIT),
        name="join",
        cost_estimate=cost(512 * mine.size),
    )(core[None], mine, other)


def turn_kernel(owners_ref, x_ref, out_ref, turned_ref, *, slots, rows):
    turned_ref[...] = x_ref[...].T
    for slot in range(slots):
        start = pl.multiple_of(owners_ref[slot] * rows, 16)
        out_ref[slot, 0] = turned_ref[pl.ds(start, rows)]


def turn(x, owners, planes):
    tokens, width = x.shape
    slots = len(owners)
    plane = width // planes
    rows = plane // slots
    if plane % 128 or rows % 16:
        blocks = x.T.reshape(planes, slots, rows, tokens)
        picked = [lax.dynamic_slice_in_dim(blocks, owner, 1, axis=1) for owner in owners]
        return jnp.concatenate(picked, axis=1).transpose(1, 0, 2, 3).reshape(width, tokens)
    return pl.pallas_call(
        functools.partial(turn_kernel, slots=slots, rows=rows),
        grid=(planes,),
        in_specs=[
            pl.BlockSpec(memory_space=pltpu.SMEM),
            pl.BlockSpec((tokens, plane), lambda p: (0, p)),
        ],
        out_specs=pl.BlockSpec((slots, 1, rows, tokens), lambda p: (0, p, 0, 0)),
        out_shape=jax.ShapeDtypeStruct((slots, planes, rows, tokens), x.dtype),
        scratch_shapes=[pltpu.VMEM((plane, tokens), x.dtype)],
        compiler_params=pltpu.CompilerParams(vmem_limit_bytes=VMEM_LIMIT),
        name="turn",
        cost_estimate=cost(512 * x.size),
    )(jnp.stack(owners), x).reshape(width, tokens)


def turn_team_kernel(*refs):
    out_ref = refs[-1]
    for number, ref in enumerate(refs[:-1]):
        rows = ref.shape[0]
        out_ref[:, number * rows : (number + 1) * rows] = ref[...].T


def turn_team(blocks):
    rows, width = blocks[0].shape
    tile = tile_of(width, 256)
    tokens = rows * len(blocks)
    return pl.pallas_call(
        turn_team_kernel,
        grid=(width // tile,),
        in_specs=[pl.BlockSpec((rows, tile), lambda j: (0, j))] * len(blocks),
        out_specs=pl.BlockSpec((tile, tokens), lambda j: (j, 0)),
        out_shape=jax.ShapeDtypeStruct((width, tokens), blocks[0].dtype),
        compiler_params=pltpu.CompilerParams(vmem_limit_bytes=VMEM_LIMIT),
        name="turn_team",
        cost_estimate=cost(512 * tokens * width),
    )(*blocks)


def place_kernel(at_ref, *refs, cuts, outs):
    sources, out_refs, sems = refs[: -1 - outs], refs[-1 - outs : -1], refs[-1]
    copies = []
    for number, (source, start, rows, of, column, wide) in enumerate(cuts):
        row_to = pl.multiple_of(at_ref[0, number], 16)
        column_to = pl.multiple_of(at_ref[1, number], 128)
        copies.append(
            pltpu.make_async_copy(
                sources[source].at[pl.ds(start, rows), pl.ds(column, wide)],
                out_refs[of].at[pl.ds(row_to, rows), pl.ds(column_to, wide)],
                sems.at[number],
            )
        )
    for copy in copies:
        copy.start()
    for copy in copies:
        copy.wait()


def place(sources, cuts, shapes):
    low = sources[0].dtype
    if any(cut[1] % 16 or cut[2] % 16 or cut[4] % 128 or cut[5] % 128 for cut in cuts):
        outs = [jnp.zeros(shape, low) for shape in shapes]
        for source, start, rows, of, column, wide, row_to, column_to in cuts:
            part = sources[source][start : start + rows, column : column + wide]
            outs[of] = lax.dynamic_update_slice(outs[of], part, (row_to, column_to))
        return outs
    places = jnp.stack(
        [jnp.stack([jnp.asarray(cut[k], jnp.int32) for cut in cuts]) for k in (6, 7)]
    )
    return pl.pallas_call(
        functools.partial(place_kernel, cuts=[cut[:6] for cut in cuts], outs=len(shapes)),
        in_specs=[pl.BlockSpec(memory_space=pltpu.SMEM)]
        + [pl.BlockSpec(memory_space=pl.ANY)] * len(sources),
        out_specs=[pl.BlockSpec(memory_space=pltpu.VMEM)] * len(shapes),
        out_shape=[jax.ShapeDtypeStruct(shape, low) for shape in shapes],
        scratch_shapes=[pltpu.SemaphoreType.DMA((len(cuts),))],
        compiler_params=pltpu.CompilerParams(vmem_limit_bytes=VMEM_LIMIT),
        name="place",
        cost_estimate=cost(512 * sum(a * b for a, b in shapes)),
    )(places, *sources)


def tile_of(size, most):
    for count in range(1, size // 128 + 1):
        if size % count == 0 and size // count % 128 == 0 and size // count <= most:
            return size // count
    return size


def product_kernel(*refs, pairs, across, kind):
    total = None
    for number in range(pairs):
        left, right = refs[2 * number][...], refs[2 * number + 1][...]
        term = dot_nt(left, right) if across else dot_nn(left, right)
        total = term if total is None else total + term
    outs = refs[2 * pairs :]
    if kind == "team":
        rows = outs[0].shape[0]
        outs[0][...] = total[:rows]
        outs[1][...] = total[rows : 2 * rows]
        outs[2][...] = total[2 * rows :].astype(jnp.bfloat16)
    else:
        outs[0][...] = total.astype(outs[0].dtype)


def product(lefts, rights, across=False, kind="low", most=256):
    rows = lefts[0].shape[0]
    wide = rights[0].shape[0 if across else 1]
    tile = tile_of(wide, most)
    operands, specs = [], []
    for left, right in zip(lefts, rights):
        depth = left.shape[1]
        operands += [left, right]
        specs.append(pl.BlockSpec((rows, depth), lambda j: (0, 0)))
        if across:
            specs.append(pl.BlockSpec((tile, depth), lambda j: (j, 0)))
        else:
            specs.append(pl.BlockSpec((depth, tile), lambda j: (0, j)))
    if kind == "team":
        shapes = [(rows // 4, jnp.float32), (rows // 4, jnp.float32), (rows // 2, jnp.bfloat16)]
    else:
        shapes = [(rows, jnp.bfloat16 if kind == "low" else jnp.float32)]
    outs = pl.pallas_call(
        functools.partial(product_kernel, pairs=len(lefts), across=across, kind=kind),
        grid=(wide // tile,),
        in_specs=specs,
        out_specs=[pl.BlockSpec((size, tile), lambda j: (0, j)) for size, _ in shapes],
        out_shape=[jax.ShapeDtypeStruct((size, wide), kept) for size, kept in shapes],
        compiler_params=pltpu.CompilerParams(vmem_limit_bytes=VMEM_LIMIT),
        name="product",
        cost_estimate=cost(2 * rows * depth * wide * len(lefts)),
    )(*operands)
    return outs if kind == "team" else outs[0]


def column_slot_kernel(at_ref, left_ref, *refs, count, added):
    left = left_ref[...]
    depth = left.shape[1] // count
    total = None
    for number in range(count):
        term = dot_nn(left[:, number * depth : (number + 1) * depth], refs[number][...])
        total = term if total is None else total + term
    for ref in refs[count : count + added]:
        total = total + ref[...].astype(jnp.float32)
    refs[-1][...] = total.astype(jnp.bfloat16)


def column_slots(left, blocks, owners, wide, added=()):
    rows = left.shape[0]
    if wide % 128:
        whole = jnp.concatenate(blocks, axis=0)
        value = jnp.concatenate(
            [nn(left, lax.dynamic_slice_in_dim(whole, owner * wide, wide, axis=1)) for owner in owners],
            axis=1,
        )
        for array, first in added:
            value = value + array[:, first * wide : (first + len(owners)) * wide].astype(jnp.float32)
        return value.astype(jnp.bfloat16)
    tile = tile_of(wide, 512)
    per = wide // tile
    return pl.pallas_call(
        functools.partial(column_slot_kernel, count=len(blocks), added=len(added)),
        grid_spec=pltpu.PrefetchScalarGridSpec(
            num_scalar_prefetch=1,
            grid=(len(owners) * per,),
            in_specs=[pl.BlockSpec(left.shape, lambda j, at: (0, 0))]
            + [
                pl.BlockSpec((block.shape[0], tile), lambda j, at: (0, at[j // per] * per + j % per))
                for block in blocks
            ]
            + [
                pl.BlockSpec((rows, tile), lambda j, at, first=first: (0, first * per + j))
                for _, first in added
            ],
            out_specs=pl.BlockSpec((rows, tile), lambda j, at: (0, j)),
        ),
        out_shape=jax.ShapeDtypeStruct((rows, len(owners) * wide), jnp.bfloat16),
        compiler_params=pltpu.CompilerParams(vmem_limit_bytes=VMEM_LIMIT),
        name="column_slots",
        cost_estimate=cost(2 * left.size * wide * len(owners)),
    )(jnp.stack(owners), left, *blocks, *[array for array, _ in added])


def packed_slot_kernel(row_ref, at_ref, turned_ref, grad_ref, context_ref, branch_ref, *refs):
    out_ref = refs[-1]
    first = dot_nn(turned_ref[...], grad_ref[...])
    second = dot_nn(context_ref[...], branch_ref[...])
    wide = first.shape[1]
    for ref in refs[:-1]:
        first = first + ref[:, :wide].astype(jnp.float32)
        second = second + ref[:, wide:].astype(jnp.float32)
    out_ref[:, :wide] = first.astype(jnp.bfloat16)
    out_ref[:, wide:] = second.astype(jnp.bfloat16)


def packed_slots(turned, grad, context, branch, slots, owners, reps, planes, added=()):
    rows = turned.shape[0] // reps
    columns = branch.shape[1] // reps
    fold = context.shape[0] // rows
    wide = grad.shape[1] + fold * columns
    if fold != 1 or columns % 128:
        outs = []
        for slot, owner in zip(slots, owners):
            first = nn(turned[slot * rows : (slot + 1) * rows], grad)
            second = nn(context, lax.dynamic_slice_in_dim(branch, owner * columns, columns, axis=1))
            outs.append(jnp.concatenate([first, folded(second, planes, fold)], axis=1))
        value = jnp.concatenate(outs, axis=0)
        for array, start in added:
            value = value + array[start * rows :][: value.shape[0]].astype(jnp.float32)
        return value.astype(jnp.bfloat16)
    block = lambda start: pl.BlockSpec((rows, wide), lambda i, row, at: (start + i, 0))
    return pl.pallas_call(
        packed_slot_kernel,
        grid_spec=pltpu.PrefetchScalarGridSpec(
            num_scalar_prefetch=2,
            grid=(len(slots),),
            in_specs=[
                pl.BlockSpec((rows, turned.shape[1]), lambda i, row, at: (row[i], 0)),
                pl.BlockSpec(grad.shape, lambda i, row, at: (0, 0)),
                pl.BlockSpec(context.shape, lambda i, row, at: (0, 0)),
                pl.BlockSpec((branch.shape[0], columns), lambda i, row, at: (0, at[i])),
            ]
            + [block(start) for _, start in added],
            out_specs=block(0),
        ),
        out_shape=jax.ShapeDtypeStruct((len(slots) * rows, wide), jnp.bfloat16),
        compiler_params=pltpu.CompilerParams(vmem_limit_bytes=VMEM_LIMIT),
        name="packed_slots",
        cost_estimate=cost(2 * len(slots) * rows * turned.shape[1] * wide),
    )(
        jnp.array(slots, jnp.int32),
        jnp.stack(owners),
        turned,
        grad,
        context,
        branch,
        *[array for array, _ in added],
    )


def folded(value, planes, fold):
    rows, wide = value.shape
    split = value.reshape(planes, fold, rows // (planes * fold), wide)
    return split.transpose(0, 2, 1, 3).reshape(rows // fold, fold * wide)


def unfolded(value, fold):
    rows, wide = value.shape
    return value.reshape(rows, fold, wide // fold).transpose(1, 0, 2).reshape(rows * fold, -1)


GELU_RATE = 0.7978845608028654
GELU_CUBE = 0.044715


def gated_kernel(*refs, count):
    gate_ref, up_ref, hidden_ref, turned_ref, gate_slope_ref, up_slope_ref = refs[count:]
    for number in range(count):
        x = refs[number][...]
        rows = x.shape[0]
        at = slice(number * rows, (number + 1) * rows)
        gate = dot_nn(x, gate_ref[...])
        up = dot_nn(x, up_ref[...])
        square = gate * gate
        bent = jnp.tanh(GELU_RATE * gate * (1.0 + GELU_CUBE * square))
        share = 0.5 * (1.0 + bent)
        gelu = gate * share
        slope = share + 0.5 * gate * (1.0 - bent * bent) * (
            GELU_RATE * (1.0 + 3.0 * GELU_CUBE * square)
        )
        hidden = (gelu * up).astype(jnp.bfloat16)
        hidden_ref[at] = hidden
        turned_ref[:, at] = hidden.T
        gate_slope_ref[at] = (slope * up).astype(jnp.bfloat16)
        up_slope_ref[at] = gelu.astype(jnp.bfloat16)


def gated(blocks, f_both):
    rows, depth = blocks[0].shape
    tokens = rows * len(blocks)
    wide = f_both.shape[1] // 2
    tile = tile_of(wide, 256)
    steps = wide // tile
    out = pl.BlockSpec((tokens, tile), lambda j: (0, j))
    kept = jax.ShapeDtypeStruct((tokens, wide), jnp.bfloat16)
    return pl.pallas_call(
        functools.partial(gated_kernel, count=len(blocks)),
        grid=(steps,),
        in_specs=[pl.BlockSpec((rows, depth), lambda j: (0, 0))] * len(blocks)
        + [
            pl.BlockSpec((depth, tile), lambda j: (0, j)),
            pl.BlockSpec((depth, tile), lambda j: (0, steps + j)),
        ],
        out_specs=[out, pl.BlockSpec((tile, tokens), lambda j: (j, 0)), out, out],
        out_shape=[kept, jax.ShapeDtypeStruct((wide, tokens), jnp.bfloat16), kept, kept],
        compiler_params=pltpu.CompilerParams(vmem_limit_bytes=VMEM_LIMIT),
        name="gated",
        cost_estimate=cost(4 * tokens * depth * wide),
    )(*blocks, f_both, f_both)


def gated_back_kernel(*refs, count):
    down_ref, gate_slope_ref, up_slope_ref, out_ref = refs[count:]
    for number in range(count):
        rows = refs[number].shape[0]
        at = slice(number * rows, (number + 1) * rows)
        d_hidden = dot_nt(refs[number][...], down_ref[...])
        out_ref[0, at] = (d_hidden * gate_slope_ref[at].astype(jnp.float32)).astype(jnp.bfloat16)
        out_ref[1, at] = (d_hidden * up_slope_ref[at].astype(jnp.float32)).astype(jnp.bfloat16)


def gated_back(blocks, f_down, gate_slope, up_slope):
    rows, depth = blocks[0].shape
    tokens = rows * len(blocks)
    wide = f_down.shape[0]
    tile = tile_of(wide, 512)
    column = pl.BlockSpec((tokens, tile), lambda j: (0, j))
    return pl.pallas_call(
        functools.partial(gated_back_kernel, count=len(blocks)),
        grid=(wide // tile,),
        in_specs=[pl.BlockSpec((rows, depth), lambda j: (0, 0))] * len(blocks)
        + [pl.BlockSpec((tile, depth), lambda j: (j, 0)), column, column],
        out_specs=pl.BlockSpec((2, tokens, tile), lambda j: (0, 0, j)),
        out_shape=jax.ShapeDtypeStruct((2, tokens, wide), jnp.bfloat16),
        compiler_params=pltpu.CompilerParams(vmem_limit_bytes=VMEM_LIMIT),
        name="gated_back",
        cost_estimate=cost(2 * tokens * depth * wide),
    )(*blocks, f_down, gate_slope, up_slope)


def pair_grad_kernel(left_ref, right_ref, out_ref):
    out_ref[...] = dot_nn(left_ref[...], right_ref[0]).astype(jnp.bfloat16)


def pair_grad(left, pair):
    rows, depth = left.shape
    wide = pair.shape[2]
    tile = tile_of(wide, 512)
    steps = wide // tile
    return pl.pallas_call(
        pair_grad_kernel,
        grid=(2 * steps,),
        in_specs=[
            pl.BlockSpec((rows, depth), lambda j: (0, 0)),
            pl.BlockSpec((1, depth, tile), lambda j: (j // steps, 0, j % steps)),
        ],
        out_specs=pl.BlockSpec((rows, tile), lambda j: (0, j)),
        out_shape=jax.ShapeDtypeStruct((rows, 2 * wide), jnp.bfloat16),
        compiler_params=pltpu.CompilerParams(vmem_limit_bytes=VMEM_LIMIT),
        name="pair_grad",
        cost_estimate=cost(4 * rows * depth * wide),
    )(left, pair)


def pair_back_kernel(pair_ref, right_ref, own_ref, side_ref, sent_ref):
    wide = pair_ref.shape[2]
    rows = own_ref.shape[0]
    right = right_ref[...]
    total = dot_nt(pair_ref[0], right[:, :wide]) + dot_nt(pair_ref[1], right[:, wide:])
    own_ref[...] = total[:rows]
    side_ref[...] = total[rows : 2 * rows]
    sent_ref[...] = total[2 * rows :].astype(jnp.bfloat16)


def pair_back(pair, f_both):
    tokens, wide = pair.shape[1:]
    width = f_both.shape[0]
    tile = tile_of(width, 512)
    shapes = [(tokens // 4, jnp.float32), (tokens // 4, jnp.float32), (tokens // 2, jnp.bfloat16)]
    return pl.pallas_call(
        pair_back_kernel,
        grid=(width // tile,),
        in_specs=[
            pl.BlockSpec(pair.shape, lambda j: (0, 0, 0), pipeline_mode=pl.Buffered(1)),
            pl.BlockSpec((tile, 2 * wide), lambda j: (j, 0)),
        ],
        out_specs=[pl.BlockSpec((size, tile), lambda j: (0, j)) for size, _ in shapes],
        out_shape=[jax.ShapeDtypeStruct((size, width), kept) for size, kept in shapes],
        compiler_params=pltpu.CompilerParams(vmem_limit_bytes=VMEM_LIMIT),
        name="pair_back",
        cost_estimate=cost(4 * tokens * wide * width),
    )(pair, f_both)


def norm_back(upstream, unit_rows, scale_rows, gain_rows):
    scaled = upstream * gain_rows
    return scale_rows * (scaled - unit_rows * jnp.mean(scaled * unit_rows, axis=-1, keepdims=True))


def tied(value, *after):
    return lax.optimization_barrier((value, *after))[0]


class Order:
    def __init__(self):
        self.last = ()

    def __call__(self, value, *after):
        return tied(value, *self.last, *after) if self.last or after else value

    def mark(self, value):
        self.last = (value,)
        return value


class Links:
    def __init__(self, reps, group):
        self.reps, self.group, self.planes = reps, group, group // 2
        self.team, self.wing, self.plane, self.core = map(lax.axis_index, AXES)
        self.q = 2 * self.team + self.wing
        self.place = 2 * self.plane + self.core

    def move(self, value, target):
        pairs = []
        for r in range(self.reps):
            for s in range(self.group):
                to_r, to_s = target(r, s)
                pairs.append((r * self.group + s, to_r * self.group + to_s))
        return lax.ppermute(value, AXES, pairs)

    def across(self, value):
        return self.move(value, lambda r, s: (r, s ^ 1))

    def sideways(self, value):
        return self.move(value, lambda r, s: (r ^ 1, s))

    def along(self, value, step):
        return self.move(value, lambda r, s: (r, (s + 2 * step) % self.group))

    def along_parts(self, value, rows):
        parts = [lax.dynamic_slice_in_dim(value, self.plane * rows, rows)]
        for step in range(1, self.planes):
            to = (self.plane + step) % self.planes
            parts.append(self.along(lax.dynamic_slice_in_dim(value, to * rows, rows), step))
        return parts

    def along_steps(self, share):
        return [self.along(share, k) for k in range(1, self.planes)]

    def spread_steps(self):
        steps = [(0, 1 << k) for k in range(self.group.bit_length() - 1)]
        steps += [(1 << k, 0) for k in range(self.reps.bit_length() - 1)]
        return [
            lambda value, r_step=r_step, s_step=s_step: self.move(
                value, lambda r, s: (r ^ r_step, s ^ s_step)
            )
            for r_step, s_step in steps
        ]


class Spread:
    def __init__(self, links, low):
        self.links, self.low = links, low
        self.count = links.reps >> low
        self.stages = self.count.bit_length() - 1
        self.own = links.q >> low

    def bit_of(self, stage, core):
        return 1 << (stage if core == 0 else self.stages - 1 - stage)

    def swap(self, value, stage):
        return self.links.move(
            value, lambda r, s: (r ^ (self.bit_of(stage, s % 2) << self.low), s)
        )

    def bit(self, stage):
        return jnp.where(self.links.core == 0, self.bit_of(stage, 0), self.bit_of(stage, 1))

    def gathered(self, value):
        parts, offsets = [value], [jnp.int32(0)]
        for stage in range(self.stages):
            parts += [self.swap(part, stage) for part in parts]
            offsets += [offset ^ self.bit(stage) for offset in offsets]
        return parts, [self.own ^ offset for offset in offsets]

    def gather_steps(self, value):
        parts, offsets = [value], [jnp.int32(0)]
        for stage in range(self.stages):
            added = [self.swap(part, stage) for part in parts]
            parts, offsets = parts + added, offsets + [offset ^ self.bit(stage) for offset in offsets]
            yield parts, [self.own ^ offset for offset in offsets]

    def turned_slot(self, slot):
        return sum(((slot >> k) & 1) << (self.stages - 1 - k) for k in range(self.stages))

    def slot_owners(self):
        owners = []
        for slot in range(self.count):
            owner = self.own
            for stage in range(self.stages):
                if (slot >> (self.stages - 1 - stage)) & 1:
                    owner = owner ^ self.bit(stage)
            owners.append(owner)
        return owners


def pick(blocks, index):
    value = blocks[0]
    for k in range(1, len(blocks)):
        value = jnp.where(index == k, blocks[k], value)
    return value


def in_order(first, parts, owners):
    parts = [parts[0] if first is None else first] + parts[1:]
    ordered = []
    for k in range(len(parts)):
        value = parts[0]
        for part, owner in zip(parts[1:], owners[1:]):
            value = jnp.where(owner == k, part, value)
        ordered.append(value)
    return ordered


def nn(left, right):
    return jnp.dot(left, right, preferred_element_type=jnp.float32)


def layer(
    reps,
    group,
    tokens,
    lengths,
    buckets,
    w_query,
    w_key,
    w_value,
    w_out,
    w_gate,
    w_up,
    w_down,
    bias_table,
    norm_attn,
    norm_ffn,
    cotangent,
):
    links = Links(reps, group)
    planes, core, plane, wing, q = links.planes, links.core, links.plane, links.wing, links.q
    spread, team = Spread(links, 0), Spread(links, 1)
    first_core = core == 0
    length, width = tokens.shape
    shard_rows, inner = w_query.shape
    head_count = bias_table.shape[1]
    head_size = inner // head_count
    bucket_count = bias_table.shape[0] * group
    half = inner // 2
    piece = w_down.shape[0] // 2
    unit = max(128, 16 * team.count)
    padded = (piece + unit - 1) // unit * unit
    at = jnp.stack([wing, core])
    share_rows = 2 * shard_rows // reps
    team_rows = 2 * shard_rows // team.count
    down_rows = padded // team.count
    out_rows = w_out.shape[0]
    fold = out_rows // share_rows
    order = Order()
    mark = order.mark

    def by_core(zero, one):
        return jnp.where(first_core, zero, one)

    def row_share(over, keep, recv):
        rows = 2 * shard_rows // over.count
        per = max(over.count // 2, 1)
        return lax.dynamic_slice_in_dim(
            jnp.where(over.own // per == core, keep, recv), over.own % per * rows, rows
        )

    def plane_of(step):
        return (plane + planes - step) % planes

    def column_half(side):
        return jnp.concatenate(
            [w[:, side * half : (side + 1) * half] for w in (w_query, w_key, w_value)], axis=1
        )

    half_zero, half_one = column_half(0), column_half(1)
    qkv_keep, qkv_send = by_core(half_zero, half_one), by_core(half_one, half_zero)
    qkv_recv = links.across(mark(qkv_send))
    ffn_keep, ffn_send = split_columns(at, order(w_gate), w_up, piece, padded)
    ffn_recv = links.across(mark(ffn_send))
    columns = width // reps
    out_share = pick([w_out[:, k * columns : (k + 1) * columns] for k in range(reps)], q)
    out_share = folded(out_share, 1, fold)
    packed_share = jnp.concatenate(
        [row_share(spread, order(qkv_keep), qkv_recv), out_share], axis=1
    )
    packed_steps = links.along_steps(mark(packed_share))
    small = jnp.concatenate([norm_attn, norm_ffn, bias_table.reshape(-1)])
    small_size = small.shape[0]
    small = jnp.pad(small, (0, -small_size % 1024)).reshape(-1, 128)
    small = mark(order(small))
    small_steps = links.along_steps(small)

    floats_in = order(tokens).astype(jnp.float32)
    scale_one = mark(
        lax.rsqrt(jnp.mean(floats_in * floats_in, axis=-1, keepdims=True) + EPSILON)
    )
    down_half = jnp.pad(
        lax.dynamic_slice_in_dim(order(w_down), wing * piece, piece), ((0, padded - piece), (0, 0))
    )
    down_share = mark(lax.dynamic_slice_in_dim(down_half, team.own * down_rows, down_rows))
    positions = lax.broadcasted_iota(jnp.int32, (bucket_count, buckets.shape[0] + 1), 0)
    turned_buckets = jnp.concatenate([order(buckets)[::-1], jnp.full((1,), -1, jnp.int32)])
    one_hot = mark((turned_buckets[None, :] == positions).astype(jnp.float32))

    small = mark(jnp.stack([order(small)] + small_steps))
    small_recv = links.across(small)
    packed_others = mark(jnp.concatenate([order(packed_steps[0])] + packed_steps[1:], axis=0))
    packed_shares, packed_owners = spread.gathered(packed_others)
    ffn_share = mark(row_share(team, order(ffn_keep), ffn_recv))
    f_ffn = lax.all_gather(ffn_share, ("plane", "team"), axis=0, tiled=True)
    f_down = lax.all_gather(
        tied(down_share, ffn_share), ("plane", "team"), axis=0, tiled=True
    )

    small = jnp.stack([order(small), small_recv])
    small = by_core(small, small[::-1])
    small = jnp.concatenate([small, small], axis=1)[:, ::-1]
    small = lax.dynamic_slice_in_dim(small, planes - 1 - plane, planes, axis=1)
    small = small.transpose(1, 0, 2, 3).reshape(group, -1)[:, :small_size]
    gain_one = small[:, :shard_rows].reshape(1, width).astype(jnp.float32)
    gain_two = small[:, shard_rows : 2 * shard_rows].reshape(1, width).astype(jnp.float32)
    full_table = small[:, 2 * shard_rows :].reshape(bucket_count, head_count)
    rel_bias = lax.dot_general(
        full_table.astype(jnp.float32),
        one_hot,
        (((0,), (0,)), ((), ())),
        precision=lax.Precision.HIGHEST,
    )
    bias_rows = mark(rel_bias.reshape(head_count // 2, 2, -1))
    normed_one = mark((order(floats_in) * scale_one * gain_one).astype(jnp.bfloat16))
    one_turned = mark(turn(normed_one, spread.slot_owners(), planes))

    wide = 3 * half
    cuts = [
        (0, 0, shard_rows, 0, 0, wide, (2 * plane + core) * shard_rows, 0),
        (1, 0, shard_rows, 0, 0, wide, (2 * plane + 1 - core) * shard_rows, 0),
        (2, 0, out_rows, 1, 0, width, plane * out_rows, 0),
    ]
    for number, owner in enumerate(packed_owners):
        for step in range(1, planes):
            start = (step - 1) * share_rows
            to = plane_of(step)
            row = to * 2 * shard_rows + owner * share_rows
            cuts.append((number + 3, start, share_rows, 0, 0, wide, row, 0))
            for k in range(fold):
                row = to * out_rows + k * share_rows
                cuts.append(
                    (
                        number + 3,
                        start,
                        share_rows,
                        1,
                        wide + k * columns,
                        columns,
                        row,
                        owner * columns,
                    )
                )
    qkv_half, out_mine = place(
        [order(qkv_keep), qkv_recv, w_out] + packed_shares,
        cuts,
        [(width, wide), (planes * out_rows, width)],
    )
    mark(qkv_half)
    qkv_other = links.across(qkv_half)
    out_theirs = links.across(out_mine)
    g_side = links.sideways(tied(cotangent, one_turned))
    own_qkv = mark(product([order(normed_one)], [qkv_half], most=384))
    other_qkv = mark(product([order(normed_one)], [qkv_other], most=384))
    qkv = mark(jnp.stack([by_core(order(own_qkv), other_qkv), by_core(other_qkv, own_qkv)]))
    context, context_turned, lse = run_forward(
        lengths, bias_rows, order(qkv), head_size
    )
    mark(context)
    (f_out,) = place(
        [order(out_mine), out_theirs],
        [
            (
                side,
                p * out_rows,
                out_rows,
                0,
                0,
                width,
                (2 * p + (core if side == 0 else 1 - core)) * out_rows,
                0,
            )
            for side in (0, 1)
            for p in range(planes)
        ],
        [(inner, width)],
    )
    attended = floats_in + nn(context, f_out)
    scale_two = lax.rsqrt(jnp.mean(attended * attended, axis=-1, keepdims=True) + EPSILON)
    unit_two = attended * scale_two
    normed_two = mark((unit_two * gain_two).astype(jnp.bfloat16))

    side_two = links.sideways(order(normed_two, g_side))
    core_two = links.across(normed_two)
    by_sides = context_turned.reshape(planes, 2, out_rows, length)
    context_own = by_core(order(by_sides)[:, 0], by_sides[:, 1]).reshape(-1, length)
    context_other = by_core(by_sides[:, 1], by_sides[:, 0]).reshape(-1, length)
    mark(context_own)
    g_core = links.across(order(cotangent))
    g_both = links.across(order(g_side))
    team_g = [cotangent, g_side, g_core, g_both]
    both_two = links.across(order(side_two))
    team_two = [normed_two, side_two, core_two, both_two]
    mark(order(both_two))
    hidden, hidden_turned, gate_slope, up_slope = gated([order(normed_two)] + team_two[1:], f_ffn)
    mark(hidden)

    two_turned = mark(turn_team([order(normed_two)] + team_two[1:]))
    d_pair = mark(gated_back([order(cotangent)] + team_g[1:], f_down, gate_slope, up_slope))
    d_own, d_side, d_sent = pair_back(order(d_pair), f_ffn)
    d_recv = links.across(mark(d_sent))

    d_side = mark((order(d_side) + d_recv[length:].astype(jnp.float32)).astype(jnp.bfloat16))
    d_theirs = links.sideways(d_side)
    ffn_sum = lax.psum_scatter(
        mark(pair_grad(order(two_turned), d_pair)),
        ("plane", "team"),
        scatter_dimension=0,
        tiled=True,
    )
    ffn_own, ffn_side, ffn_sent = product([order(hidden)], [f_down], kind="team")
    ffn_their = links.across(mark(ffn_sent))

    d_normed_two = (
        order(d_own) + d_recv[:length].astype(jnp.float32) + d_theirs.astype(jnp.float32)
    )
    ffn_gain_term = jnp.sum(d_normed_two * unit_two, axis=0)
    grad_in = cotangent.astype(jnp.float32)
    d_attended = grad_in + norm_back(d_normed_two, unit_two, scale_two, gain_two)
    d_branch = d_attended.astype(jnp.bfloat16)
    d_context = mark(product([d_branch], [f_out], across=True))
    ffn_side = mark((order(ffn_side) + ffn_their[length:].astype(jnp.float32)).astype(jnp.bfloat16))
    ffn_theirs = links.sideways(ffn_side)

    d_query, d_key, d_value, d_lined = run_backward(
        lengths, bias_rows, qkv, tied(d_context, ffn_side), lse, head_size
    )
    d_qkv = mark(jnp.concatenate([d_query, d_key, d_value], axis=2))
    d_mine = by_core(order(d_qkv)[0], d_qkv[1])
    d_other = by_core(d_qkv[1], d_qkv[0])
    owners = spread.slot_owners()
    d_normed_one = product(
        [order(d_mine), d_other], [qkv_half, qkv_other], across=True, kind="wide"
    )
    unit_one = floats_in * scale_one
    attn_gain_term = jnp.sum(d_normed_one * unit_one, axis=0)
    grad_tokens = mark(
        (d_attended + norm_back(d_normed_one, unit_one, scale_one, gain_one)).astype(jnp.bfloat16)
    )
    table_term = lax.dot_general(
        one_hot,
        order(d_lined).reshape(head_count, -1),
        (((1,), (1,)), ((), ())),
        precision=lax.Precision.HIGHEST,
    )
    terms = jnp.concatenate([attn_gain_term, ffn_gain_term, table_term.reshape(-1)])
    terms = mark(jnp.pad(terms, (0, -terms.shape[0] % 1024)).reshape(-1, 128))
    output = mark(
        (
            order(attended)
            + ffn_own
            + ffn_their[:length].astype(jnp.float32)
            + ffn_theirs.astype(jnp.float32)
        ).astype(jnp.bfloat16)
    )

    def packed(slots, grad, context_rows, added):
        return mark(
            packed_slots(
                one_turned,
                order(grad),
                context_rows,
                d_branch,
                slots,
                [owners[slot] for slot in slots],
                reps,
                planes,
                added,
            )
        )

    exchanges = links.spread_steps()

    def summed_on():
        nonlocal terms
        terms = mark(order(terms) + arrived_terms)

    back = packed([spread.turned_slot(slot) for slot in range(reps)], d_other, context_other, [])
    arrived_terms = exchanges.pop(0)(terms)
    arrived = [links.across(back)]
    low, high = reps // 2, reps
    for stage in range(spread.stages):
        summed_on()
        sent = packed(range(low, high), d_mine, context_own, [(value, low) for value in arrived])
        arrived_terms = exchanges.pop(0)(terms)
        arrived.append(spread.swap(sent, stage))
        if stage == 0:
            down_sum = lax.psum_scatter(
                mark(
                    column_slots(
                        order(hidden_turned), team_g, [jnp.int32(k) for k in range(reps)], width // reps
                    )
                ),
                ("plane", "team"),
                scatter_dimension=0,
                tiled=True,
            )
            order.last = (*order.last, ffn_sum)
        low, high = low // 2, low
    summed_on()
    sent = packed([0], d_mine, context_own, [(value, 0) for value in arrived])
    packed_parts = links.along_parts(sent, share_rows)
    ffn_steps = spread.gather_steps(order(ffn_sum))
    ffn_shares = next(ffn_steps)
    came = exchanges.pop(0)(terms)
    packed_total = mark(
        sum(
            part.astype(jnp.float32)
            for part in [order(packed_parts[0], ffn_shares[0][1])] + packed_parts[1:]
        ).astype(jnp.bfloat16)
    )
    packed_shares = spread.gathered(packed_total)
    for ffn_shares in ffn_steps:
        pass
    terms = tied(terms, packed_total) + came
    came = exchanges.pop(0)(terms)
    down_shares = spread.gathered(tied(down_sum, packed_shares[0][1]))
    terms = tied(terms, *packed_shares[0]) + came
    for exchange in exchanges:
        terms = terms + exchange(terms)
    terms = terms.reshape(-1)

    def by_owner(parts):
        per = len(parts) // 2
        low = jnp.concatenate(parts[:per], axis=0)
        high = jnp.concatenate(parts[per:], axis=0)
        return by_core(low, high), by_core(high, low)

    def wings_apart(parts):
        return parts[0::2] + parts[1::2]

    parts = in_order(None, *down_shares)
    grad_down = jnp.concatenate(
        [jnp.concatenate(parts[w::2], axis=0)[:piece] for w in (0, 1)], axis=0
    ).astype(jnp.float32)
    parts = in_order(None, *ffn_shares)
    per = reps // 2
    low, high = wings_apart(parts[:per]), wings_apart(parts[per:])
    low, high = jnp.concatenate(low, axis=0), jnp.concatenate(high, axis=0)
    ffn_mine, ffn_send = by_core(low, high), by_core(high, low)
    ffn_other = links.across(ffn_send)
    grad_gate, grad_up = join_columns(core, ffn_mine, ffn_other, piece, padded)

    parts = in_order(None, *packed_shares)
    grad_out = jnp.concatenate(
        [unfolded(part[:, wide:], fold) for part in parts], axis=1
    ).astype(jnp.float32)
    qkv_mine, qkv_send = by_owner([part[:, :wide] for part in parts])
    qkv_recv = links.across(qkv_send)
    grad_halves = (by_core(qkv_mine, qkv_recv), by_core(qkv_recv, qkv_mine))
    grad_query, grad_key, grad_value = [
        jnp.concatenate(
            [value[:, kind * half : (kind + 1) * half] for value in grad_halves], axis=1
        ).astype(jnp.float32)
        for kind in range(3)
    ]
    grad_norm_attn = lax.dynamic_slice_in_dim(terms, links.place * shard_rows, shard_rows)
    grad_norm_ffn = lax.dynamic_slice_in_dim(terms, width + links.place * shard_rows, shard_rows)
    table_size = bias_table.size
    grad_table = lax.dynamic_slice_in_dim(
        terms, 2 * width + links.place * table_size, table_size
    ).reshape(bias_table.shape)
    return (
        output,
        grad_tokens,
        grad_query,
        grad_key,
        grad_value,
        grad_out,
        grad_gate,
        grad_up,
        grad_down,
        grad_table,
        grad_norm_attn,
        grad_norm_ffn,
    )


def solution(mesh):
    reps, group = mesh.shape["rep"], mesh.shape["shard"]
    devices = mesh.devices.reshape(reps // 2, 2, group // 2, 2)
    rows, part = P(AXES[2:], None), P(AXES[2:])
    tokens = P(AXES, None)
    return jax.shard_map(
        functools.partial(layer, reps, group),
        mesh=jax.sharding.Mesh(devices, AXES),
        in_specs=(tokens, P(AXES), P()) + (rows,) * 8 + (part, part, tokens),
        out_specs=(tokens, tokens) + (rows,) * 8 + (part, part),
        check_vma=False,
    )
```

profile of v0, /device:TPU:10, one launch (start us, length us, event | category | flops | bytes accessed | tf_op | source)
XLA Modules:
  0.0 544.7 jit_solution(18023147150428350367)
XLA Ops:
  11.2 4.7 split.1
  21.2 4.4 collective-permute-done.1
  28.8 18.0 %collective-permute-done.5 = bf16[96,1536]{1,0:T(8,128)(2,1)S(1)} collective-permute-done((bf16[96,1536]{1,0:T(8,128)(2,1)S(1)}, bf16[96,1536]{1,0:T(8,128)(2,1)S(1)}, u32[]{:S(2)}, u32[]{:S(2)}) %collective-permute-start.5) | collective-permute-done | bytes 294944 | tf_op jit(solution)/shard_map/ppermute | solution.py:686
  58.5 15.1 %collective-permute-done.9.refs_4_ = bf16[288,1536]{1,0:T(8,128)(2,1)} collective-permute-done((bf16[288,1536]{1,0:T(8,128)(2,1)}, bf16[288,1536]{1,0:T(8,128)(2,1)}, u32[]{:S(2)}, u32[]{:S(2)}) %collective-permute-start.9) | collective-permute-done | bytes 884768 | tf_op jit(solution)/shard_map/ppermute | solution.py:686
  79.1 3.9 turn.1
  83.8 9.5 %collective-permute-done.11.refs_6_ = bf16[288,1536]{1,0:T(8,128)(2,1)S(1)} collective-permute-done((bf16[288,1536]{1,0:T(8,128)(2,1)}, bf16[288,1536]{1,0:T(8,128)(2,1)S(1)}, u32[]{:S(2)}, u32[]{:S(2)}) %collective-permute-start.11) | collective-permute-done | bytes 884768 | tf_op jit(solution)/shard_map/ppermute | solution.py:686
  94.1 5.6 %place.2 = (bf16[1536,1152]{1,0:T(8,128)(2,1)}, bf16[384,1536]{1,0:T(8,128)(2,1)}) custom-call(s32[2,27]{1,0:T(2,128)} %pad_add_fusion.1.at_ref, bf16[192,1152]{1,0:T(8,128)(2,1)} %copy-done.13, bf16[192,1152]{1,0:T(8,128)(2,1)} %copy-done.24, bf16[96,1536]{1,0:T(8,128)(2,1)} %refs_2_.1, bf16[288,1536]{1,0:T(8,128)(2,1)} %copy-done.17, ...), custom_call_target="tpu_custom_call" | custom-call | flops 1207959552 | bytes 2359296 | tf_op jit(solution)/shard_map/place/pallas_call | solution.py:337
  102.6 6.0 %product.5 = bf16[512,1152]{1,0:T(8,128)(2,1)} custom-call(bf16[512,1536]{1,0:T(8,128)(2,1)} %multiply_convert_fusion.1.x_ref.refs_0_, bf16[1536,1152]{1,0:T(8,128)(2,1)} %get-tuple-element.95.refs_1_), custom_call_target="tpu_custom_call" | custom-call | flops 1811939328 | bytes 3538944 | tf_op jit(solution)/shard_map/product/pallas_call | solution.py:390
  108.9 6.1 %product.6 = bf16[512,1152]{1,0:T(8,128)(2,1)} custom-call(bf16[512,1536]{1,0:T(8,128)(2,1)} %multiply_convert_fusion.1.x_ref.refs_0_, bf16[1536,1152]{1,0:T(8,128)(2,1)} %collective-permute-done.12.refs_1_.refs_3_), custom_call_target="tpu_custom_call" | custom-call | flops 1811939328 | bytes 3538944 | tf_op jit(solution)/shard_map/product/pallas_call | solution.py:390
  118.1 10.5 %attend.1 = (bf16[512,768]{1,0:T(8,128)(2,1)}, bf16[768,512]{1,0:T(8,128)(2,1)}, f32[6,2,512]{2,1,0:T(2,128)}) custom-call(s32[1]{0:T(128)S(6)} %copy.58.valid_ref, f32[6,2,1024]{2,1,0:T(2,128)} %copy.38.bias_ref, bf16[2,512,1152]{2,1,0:T(8,128)(2,1)} %pad_maximum_fusion.q_ref.k_ref.v_ref, bf16[2,512,1152]{2,1,0:T(8,128)(2,1)} %pad_maximum_fusion.q_ref.k_ref.v_ref, ...), custom_call_target="tpu_custom_call" | custom-call | flops 3221225472 | bytes 6291456 | tf_op jit(solution)/shard_map/attend/pallas_call | solution.py:128
  129.6 3.9 place.3.refs_1_
  140.5 34.4 %collective-permute-done.15.refs_1_ = bf16[512,1536]{1,0:T(8,128)(2,1)S(1)} collective-permute-done((bf16[512,1536]{1,0:T(8,128)(2,1)S(1)}, bf16[512,1536]{1,0:T(8,128)(2,1)S(1)}, u32[]{:S(2)}, u32[]{:S(2)}) %collective-permute-start.15) | collective-permute-done | bytes 1572896 | tf_op jit(solution)/shard_map/ppermute | solution.py:686
  177.2 3.5 collective-permute-done.17.refs_3_
  180.7 22.9 %gated.1 = (bf16[2048,1024]{1,0:T(8,128)(2,1)}, bf16[1024,2048]{1,0:T(8,128)(2,1)}, bf16[2048,1024]{1,0:T(8,128)(2,1)}, bf16[2048,1024]{1,0:T(8,128)(2,1)}) custom-call(bf16[512,1536]{1,0:T(8,128)(2,1)} %copy-done.11, bf16[512,1536]{1,0:T(8,128)(2,1)} %copy-done.15, bf16[512,1536]{1,0:T(8,128)(2,1)} %copy-done.16, ...), custom_call_target="tpu_custom_call" | custom-call | flops 12884901888 | bytes 25165824 | tf_op jit(solution)/shard_map/gated/pallas_call | solution.py:553
  203.6 7.5 %turn_team.1.left_ref = bf16[1536,2048]{1,0:T(8,128)(2,1)} custom-call(bf16[512,1536]{1,0:T(8,128)(2,1)} %copy-done.11, bf16[512,1536]{1,0:T(8,128)(2,1)} %copy-done.15, bf16[512,1536]{1,0:T(8,128)(2,1)} %copy-done.16, bf16[512,1536]{1,0:T(8,128)(2,1)} %collective-permute-done.17.refs_3_), custom_call_target="tpu_custom_call" | custom-call | flops 1610612736 | bytes 3145728 | tf_op jit(solution)/shard_map/turn_team/pallas_call | solution.py:295
  211.2 5.1 all-gather.5.cloned.1.call-done.refs_4_.refs_1_
  216.3 14.4 %gated_back.1.pair_ref.right_ref = bf16[2,2048,1024]{2,1,0:T(8,128)(2,1)} custom-call(bf16[512,1536]{1,0:T(8,128)(2,1)} %refs_0_.2, bf16[512,1536]{1,0:T(8,128)(2,1)} %collective-permute-done.14.refs_1_, bf16[512,1536]{1,0:T(8,128)(2,1)} %collective-permute-done.18.refs_2_, bf16[512,1536]{1,0:T(8,128)(2,1)} %collective-permute-done.19.refs_3_, ...), custom_call_target="tpu_custom_call" | custom-call | flops 6442450944 | bytes 12582912 | tf_op jit(solution)/shard_map/gated_back/pallas_call | solution.py:585
  230.7 19.3 %pair_back.1 = (f32[512,1536]{1,0:T(8,128)}, f32[512,1536]{1,0:T(8,128)}, bf16[1024,1536]{1,0:T(8,128)(2,1)}) custom-call(bf16[2,2048,1024]{2,1,0:T(8,128)(2,1)} %gated_back.1.pair_ref.right_ref, bf16[1536,2048]{1,0:T(8,128)(2,1)} %all-gather.3.cloned.1.call-done.refs_4_.refs_5_.right_ref), custom_call_target="tpu_custom_call" | custom-call | flops 12884901888 | bytes 25165824 | tf_op jit(solution)/shard_map/pair_back/pallas_call | solution.py:637
  250.0 5.9 %collective-permute-done.20 = bf16[1024,1536]{1,0:T(8,128)(2,1)S(1)} collective-permute-done((bf16[1024,1536]{1,0:T(8,128)(2,1)}, bf16[1024,1536]{1,0:T(8,128)(2,1)S(1)}, u32[]{:S(2)}, u32[]{:S(2)}) %collective-permute-start.20) | collective-permute-done | bytes 3145760 | tf_op jit(solution)/shard_map/ppermute | solution.py:686
  255.9 4.7 add_convert_fusion.3
  261.2 18.5 %pair_grad.1 = bf16[1536,2048]{1,0:T(8,128)(2,1)} custom-call(bf16[1536,2048]{1,0:T(8,128)(2,1)} %turn_team.1.left_ref, bf16[2,2048,1024]{2,1,0:T(8,128)(2,1)} %gated_back.1.pair_ref.right_ref), custom_call_target="tpu_custom_call" | custom-call | flops 12884901888 | bytes 25165824 | tf_op jit(solution)/shard_map/pair_grad/pallas_call | solution.py:607
  279.7 10.9 %product.7 = (f32[512,1536]{1,0:T(8,128)}, f32[512,1536]{1,0:T(8,128)}, bf16[1024,1536]{1,0:T(8,128)(2,1)}) custom-call(bf16[2048,1024]{1,0:T(8,128)(2,1)} %get-tuple-element.122.refs_0_, bf16[1024,1536]{1,0:T(8,128)(2,1)} %all-gather.5.cloned.1.call-done.refs_4_.refs_1_), custom_call_target="tpu_custom_call" | custom-call | flops 6442450944 | bytes 12582912 | tf_op jit(solution)/shard_map/product/pallas_call | solution.py:390
  291.3 6.1 %collective-permute-done.21 = bf16[512,1536]{1,0:T(8,128)(2,1)} collective-permute-done((bf16[512,1536]{1,0:T(8,128)(2,1)}, bf16[512,1536]{1,0:T(8,128)(2,1)}, u32[]{:S(2)}, u32[]{:S(2)}) %collective-permute-start.21) | collective-permute-done | bytes 1572896 | tf_op jit(solution)/shard_map/ppermute | solution.py:686
  297.4 4.1 multiply_reduce_fusion.1
  301.6 5.4 fusion.20
  307.0 5.4 product.8.dctx_ref
  316.0 16.7 %attend_back.1 = (bf16[2,512,384]{2,1,0:T(8,128)(2,1)}, bf16[2,512,384]{2,1,0:T(8,128)(2,1)}, bf16[2,512,384]{2,1,0:T(8,128)(2,1)}, f32[6,2,1024]{2,1,0:T(2,128)}) custom-call(s32[1]{0:T(128)S(6)} %copy.58.valid_ref, f32[6,2,1024]{2,1,0:T(2,128)} %copy.38.bias_ref, bf16[2,512,1152]{2,1,0:T(8,128)(2,1)} %pad_maximum_fusion.q_ref.k_ref.v_ref, ...), custom_call_target="tpu_custom_call" | custom-call | flops 6442450944 | bytes 12582912 | tf_op jit(solution)/shard_map/attend_back/pallas_call | solution.py:162
  337.1 9.5 %product.9 = f32[512,1536]{1,0:T(8,128)} custom-call(bf16[512,1152]{1,0:T(8,128)(2,1)} %get-tuple-element.146.refs_0_.grad_ref, bf16[1536,1152]{1,0:T(8,128)(2,1)} %get-tuple-element.95.refs_1_, bf16[512,1152]{1,0:T(8,128)(2,1)} %get-tuple-element.138.refs_2_.grad_ref, bf16[1536,1152]{1,0:T(8,128)(2,1)} %collective-permute-done.12.refs_1_.refs_3_), custom_call_target="tpu_custom_call" | custom-call | flops 3623878656 | bytes 7077888 | tf_op jit(solution)/shard_map/product/pallas_call | solution.py:390
  349.5 3.9 add_convert_fusion.1
  353.8 4.9 add_convert_fusion
  358.8 7.7 %packed_slots.4 = bf16[1536,1536]{1,0:T(8,128)(2,1)} custom-call(s32[4]{0:T(128)} %constant.176.clone.row_ref, s32[4]{0:T(128)} %add_add_fusion.1.at_ref, bf16[1536,512]{1,0:T(8,128)(2,1)} %bitcast.89, bf16[512,1152]{1,0:T(8,128)(2,1)} %get-tuple-element.138.refs_2_.grad_ref, bf16[384,512]{1,0:T(8,128)(2,1)} %bitcast.97, ...), custom_call_target="tpu_custom_call" | custom-call | flops 2415919104 | bytes 4718592 | tf_op jit(solution)/shard_map/packed_slots/pallas_call | solution.py:479
  367.6 4.8 collective-permute-done.24
  376.8 6.0 %packed_slots.5 = bf16[768,1536]{1,0:T(8,128)(2,1)} custom-call(s32[2]{0:T(128)} %constant.177.clone.row_ref, s32[2]{0:T(128)} %pad_add_fusion.3.at_ref, bf16[1536,512]{1,0:T(8,128)(2,1)} %bitcast.90, bf16[512,1152]{1,0:T(8,128)(2,1)} %get-tuple-element.146.refs_0_.grad_ref, bf16[384,512]{1,0:T(8,128)(2,1)} %bitcast.93, ...), custom_call_target="tpu_custom_call" | custom-call | flops 1207959552 | bytes 2359296 | tf_op jit(solution)/shard_map/packed_slots/pallas_call | solution.py:479
  385.0 14.2 %column_slots.1 = bf16[1024,1536]{1,0:T(8,128)(2,1)} custom-call(s32[4]{0:T(128)} %iota.9.at_ref, bf16[1024,2048]{1,0:T(8,128)(2,1)} %get-tuple-element.142.left_ref, bf16[512,1536]{1,0:T(8,128)(2,1)} %refs_0_.2, bf16[512,1536]{1,0:T(8,128)(2,1)} %collective-permute-done.14.refs_1_, bf16[512,1536]{1,0:T(8,128)(2,1)} %collective-permute-done.18.refs_2_, ...), custom_call_target="tpu_custom_call" | custom-call | flops 6442450944 | bytes 12582912 | tf_op jit(solution)/shard_map/column_slots/pallas_call | solution.py:428
  399.5 8.3 %reduce-scatter.3.cloned.1.call-done = bf16[192,2048]{1,0:T(8,128)(2,1)} async-done(((bf16[1536,2048]{1,0:T(8,128)(2,1)}), bf16[192,2048]{1,0:T(8,128)(2,1)}) %reduce-scatter.3.cloned.1.call-update) | async-done | bytes 786448 | tf_op jit(solution)/shard_map/reduce_scatter | solution.py:989
  407.8 4.1 collective-permute-done.27.refs_1_
  413.3 4.3 packed_slots.6
  418.9 4.1 collective-permute-done.28
  423.0 18.3 %collective-permute-done.29.refs_2_ = bf16[384,1536]{1,0:T(8,128)(2,1)S(1)} collective-permute-done((bf16[384,1536]{1,0:T(8,128)(2,1)}, bf16[384,1536]{1,0:T(8,128)(2,1)S(1)}, u32[]{:S(2)}, u32[]{:S(2)}) %collective-permute-start.29) | collective-permute-done | bytes 1179680 | tf_op jit(solution)/shard_map/ppermute | solution.py:686
  442.4 4.9 packed_slots.7
  453.7 5.6 %collective-permute-done.30 = bf16[192,2048]{1,0:T(8,128)(2,1)S(1)} collective-permute-done((bf16[192,2048]{1,0:T(8,128)(2,1)S(1)}, bf16[192,2048]{1,0:T(8,128)(2,1)S(1)}, u32[]{:S(2)}, u32[]{:S(2)}) %collective-permute-start.30) | collective-permute-done | bytes 786464 | tf_op jit(solution)/shard_map/ppermute | solution.py:686
  459.3 8.9 %collective-permute-done.31 = bf16[96,1536]{1,0:T(8,128)(2,1)S(1)} collective-permute-done((bf16[96,1536]{1,0:T(8,128)(2,1)S(1)}, bf16[96,1536]{1,0:T(8,128)(2,1)S(1)}, u32[]{:S(2)}, u32[]{:S(2)}) %collective-permute-start.31) | collective-permute-done | bytes 294944 | tf_op jit(solution)/shard_map/ppermute | solution.py:686
  475.1 8.1 %collective-permute-done.34 = bf16[96,1536]{1,0:T(8,128)(2,1)S(1)} collective-permute-done((bf16[96,1536]{1,0:T(8,128)(2,1)S(1)}, bf16[96,1536]{1,0:T(8,128)(2,1)S(1)}, u32[]{:S(2)}, u32[]{:S(2)}) %collective-permute-start.34) | collective-permute-done | bytes 294944 | tf_op jit(solution)/shard_map/ppermute | solution.py:686
  490.8 7.8 %collective-permute-done.45 = f32[32,128]{1,0:T(8,128)S(1)} collective-permute-done((f32[32,128]{1,0:T(8,128)S(1)}, f32[32,128]{1,0:T(8,128)S(1)}, u32[]{:S(2)}, u32[]{:S(2)}) %collective-permute-start.45) | collective-permute-done | bytes 16416 | tf_op jit(solution)/shard_map/ppermute | solution.py:686
  503.0 4.2 collective-permute-done.38
  513.7 9.3 %collective-permute-done.41 = bf16[128,1536]{1,0:T(8,128)(2,1)S(1)} collective-permute-done((bf16[128,1536]{1,0:T(8,128)(2,1)}, bf16[128,1536]{1,0:T(8,128)(2,1)S(1)}, u32[]{:S(2)}, u32[]{:S(2)}) %collective-permute-start.41) | collective-permute-done | bytes 393248 | tf_op jit(solution)/shard_map/ppermute | solution.py:686
  525.6 5.2 collective-permute-done.42
  533.0 5.0 join.1
  (252 shorter events, 107.4 us)
Async XLA Ops:
  7.2 173.5 %all-gather.3.cloned.1.call-start = ((), (), s32[]{:S(2)}) async-start(), calls=%async_computation.2 | async-start | bytes 7077888 | tf_op jit(solution)/shard_map/all_gather | solution.py:879
  10.6 5.4 collective-permute-start
  16.1 12.6 %collective-permute-start.4 = (bf16[96,1536]{1,0:T(8,128)(2,1)S(1)}, bf16[96,1536]{1,0:T(8,128)(2,1)S(1)}, u32[]{:S(2)}, u32[]{:S(2)}) collective-permute-start(bf16[96,1536]{1,0:T(8,128)(2,1)S(1)} %pad_maximum_fusion.8), channel_id=1, source_target_pairs={{0,2},{1,3},{2,4},{3,5},{4,6},{5,7},{6,0},{7,1},{8,10},{9,11},{10,... | collective-permute-start | bytes 884744 | tf_op jit(solution)/shard_map/ppermute | solution.py:686
  17.9 7.7 %collective-permute-start.1 = (bf16[8,128]{1,0:T(8,128)(2,1)S(1)}, bf16[8,128]{1,0:T(8,128)(2,1)S(1)}, u32[]{:S(2)}, u32[]{:S(2)}) collective-permute-start(bf16[8,128]{1,0:T(8,128)(2,1)S(1)} %fusion.19), channel_id=1, source_target_pairs={{0,2},{1,3},{2,4},{3,5},{4,6},{5,7},{6,0},{7,1},{8,10},{9,11},{10,... | collective-permute-start | bytes 6152 | tf_op jit(solution)/shard_map/ppermute | solution.py:686
  19.5 8.7 %collective-permute-start.2 = (bf16[8,128]{1,0:T(8,128)(2,1)S(1)}, bf16[8,128]{1,0:T(8,128)(2,1)S(1)}, u32[]{:S(2)}, u32[]{:S(2)}) collective-permute-start(bf16[8,128]{1,0:T(8,128)(2,1)S(1)} %fusion.19), channel_id=1, source_target_pairs={{0,4},{1,5},{2,6},{3,7},{4,0},{5,1},{6,2},{7,3},{8,12},{9,13},{10,... | collective-permute-start | bytes 6152 | tf_op jit(solution)/shard_map/ppermute | solution.py:686
  20.7 8.0 %collective-permute-start.3 = (bf16[8,128]{1,0:T(8,128)(2,1)S(1)}, bf16[8,128]{1,0:T(8,128)(2,1)S(1)}, u32[]{:S(2)}, u32[]{:S(2)}) collective-permute-start(bf16[8,128]{1,0:T(8,128)(2,1)S(1)} %fusion.19), channel_id=1, source_target_pairs={{0,6},{1,7},{2,0},{3,1},{4,2},{5,3},{6,4},{7,5},{8,14},{9,15},{10,... | collective-permute-start | bytes 6152 | tf_op jit(solution)/shard_map/ppermute | solution.py:686
  21.2 27.5 %collective-permute-start.7 = (bf16[192,2048]{1,0:T(8,128)(2,1)}, bf16[192,2048]{1,0:T(8,128)(2,1)}, u32[]{:S(2)}, u32[]{:S(2)}) collective-permute-start(bf16[192,2048]{1,0:T(8,128)(2,1)} %get-tuple-element.84), channel_id=1, source_target_pairs={{0,1},{1,0},{2,3},{3,2},{4,5},{5,4},{6,7},{7,6},{8,9},{9,8},{10,11... | collective-permute-start | bytes 2359304 | tf_op jit(solution)/shard_map/ppermute | solution.py:686
  25.6 21.2 %collective-permute-start.5 = (bf16[96,1536]{1,0:T(8,128)(2,1)S(1)}, bf16[96,1536]{1,0:T(8,128)(2,1)S(1)}, u32[]{:S(2)}, u32[]{:S(2)}) collective-permute-start(bf16[96,1536]{1,0:T(8,128)(2,1)S(1)} %pad_maximum_fusion.8), channel_id=1, source_target_pairs={{0,4},{1,5},{2,6},{3,7},{4,0},{5,1},{6,2},{7,3},{8,12},{9,13},{10,... | collective-permute-start | bytes 884744 | tf_op jit(solution)/shard_map/ppermute | solution.py:686
  28.2 19.5 %collective-permute-start.6 = (bf16[96,1536]{1,0:T(8,128)(2,1)S(1)}, bf16[96,1536]{1,0:T(8,128)(2,1)S(1)}, u32[]{:S(2)}, u32[]{:S(2)}) collective-permute-start(bf16[96,1536]{1,0:T(8,128)(2,1)S(1)} %pad_maximum_fusion.8), channel_id=1, source_target_pairs={{0,6},{1,7},{2,0},{3,1},{4,2},{5,3},{6,4},{7,5},{8,14},{9,15},{10,... | collective-permute-start | bytes 884744 | tf_op jit(solution)/shard_map/ppermute | solution.py:686
  50.9 165.3 %all-gather.5.cloned.1.call-start = ((), (), s32[]{:S(2)}) async-start(), calls=%async_computation.3 | async-start | bytes 3538944 | tf_op jit(solution)/shard_map/all_gather | solution.py:880
  53.5 20.1 %collective-permute-start.9 = (bf16[288,1536]{1,0:T(8,128)(2,1)}, bf16[288,1536]{1,0:T(8,128)(2,1)}, u32[]{:S(2)}, u32[]{:S(2)}) collective-permute-start(bf16[288,1536]{1,0:T(8,128)(2,1)} %copy-done.17), channel_id=1, source_target_pairs={{0,8},{1,17},{2,10},{3,19},{4,12},{5,21},{6,14},{7,23},{8,0},{9,25... | collective-permute-start | bytes 2654216 | tf_op jit(solution)/shard_map/ppermute | solution.py:686
  57.4 26.4 %collective-permute-start.10 = (bf16[288,1536]{1,0:T(8,128)(2,1)S(1)}, bf16[288,1536]{1,0:T(8,128)(2,1)S(1)}, u32[]{:S(2)}, u32[]{:S(2)}) collective-permute-start(bf16[288,1536]{1,0:T(8,128)(2,1)S(1)} %copy-done.18), channel_id=1, source_target_pairs={{0,16},{1,9},{2,18},{3,11},{4,20},{5,13},{6,22},{7,15},{8,24},{9,1... | collective-permute-start | bytes 2654216 | tf_op jit(solution)/shard_map/ppermute | solution.py:686
  73.6 19.6 %collective-permute-start.11 = (bf16[288,1536]{1,0:T(8,128)(2,1)}, bf16[288,1536]{1,0:T(8,128)(2,1)S(1)}, u32[]{:S(2)}, u32[]{:S(2)}) collective-permute-start(bf16[288,1536]{1,0:T(8,128)(2,1)} %collective-permute-done.9.refs_4_), channel_id=1, source_target_pairs={{0,16},{1,9},{2,18},{3,11},{4,20},{5,13},{6,22},{7,15},{8,24},{9,1... | collective-permute-start | bytes 2654216 | tf_op jit(solution)/shard_map/ppermute | solution.py:686
  99.7 9.2 %collective-permute-start.12 = (bf16[1536,1152]{1,0:T(8,128)(2,1)}, bf16[1536,1152]{1,0:T(8,128)(2,1)}, u32[]{:S(2)}, u32[]{:S(2)}) collective-permute-start(bf16[1536,1152]{1,0:T(8,128)(2,1)} %get-tuple-element.95.refs_1_), channel_id=1, source_target_pairs={{0,1},{1,0},{2,3},{3,2},{4,5},{5,4},{6,7},{7,6},{8,9},{9,8},{10,11... | collective-permute-start | bytes 10616840 | tf_op jit(solution)/shard_map/ppermute | solution.py:686
  101.8 37.1 %collective-permute-start.14 = (bf16[512,1536]{1,0:T(8,128)(2,1)}, bf16[512,1536]{1,0:T(8,128)(2,1)}, u32[]{:S(2)}, u32[]{:S(2)}) collective-permute-start(bf16[512,1536]{1,0:T(8,128)(2,1)} %refs_0_.2), channel_id=1, source_target_pairs={{0,8},{1,9},{2,10},{3,11},{4,12},{5,13},{6,14},{7,15},{8,0},{9,1},... | collective-permute-start | bytes 4718600 | tf_op jit(solution)/shard_map/ppermute | solution.py:686
  102.4 305.4 %reduce-scatter.3.cloned.1.call-start = ((), (), s32[]{:S(2)}) async-start(), calls=%async_computation.4 | async-start | bytes 7077888 | tf_op jit(solution)/shard_map/reduce_scatter | solution.py:989
  108.7 19.9 %collective-permute-start.13 = (bf16[384,1536]{1,0:T(8,128)(2,1)S(1)}, bf16[384,1536]{1,0:T(8,128)(2,1)S(1)}, u32[]{:S(2)}, u32[]{:S(2)}) collective-permute-start(bf16[384,1536]{1,0:T(8,128)(2,1)S(1)} %copy-done.21), channel_id=1, source_target_pairs={{0,1},{1,0},{2,3},{3,2},{4,5},{5,4},{6,7},{7,6},{8,9},{9,8},{10,11... | collective-permute-start | bytes 3538952 | tf_op jit(solution)/shard_map/ppermute | solution.py:686
  138.9 36.0 %collective-permute-start.15 = (bf16[512,1536]{1,0:T(8,128)(2,1)S(1)}, bf16[512,1536]{1,0:T(8,128)(2,1)S(1)}, u32[]{:S(2)}, u32[]{:S(2)}) collective-permute-start(bf16[512,1536]{1,0:T(8,128)(2,1)S(1)} %multiply_convert_fusion.refs_0_), channel_id=1, source_target_pairs={{0,8},{1,9},{2,10},{3,11},{4,12},{5,13},{6,14},{7,15},{8,0},{9,1},... | collective-permute-start | bytes 4718600 | tf_op jit(solution)/shard_map/ppermute | solution.py:686
  139.5 36.0 %collective-permute-start.16 = (bf16[512,1536]{1,0:T(8,128)(2,1)S(1)}, bf16[512,1536]{1,0:T(8,128)(2,1)S(1)}, u32[]{:S(2)}, u32[]{:S(2)}) collective-permute-start(bf16[512,1536]{1,0:T(8,128)(2,1)S(1)} %multiply_convert_fusion.refs_0_), channel_id=1, source_target_pairs={{0,1},{1,0},{2,3},{3,2},{4,5},{5,4},{6,7},{7,6},{8,9},{9,8},{10,11... | collective-permute-start | bytes 4718600 | tf_op jit(solution)/shard_map/ppermute | solution.py:686
  175.0 5.8 %collective-permute-start.17 = (bf16[512,1536]{1,0:T(8,128)(2,1)S(1)}, bf16[512,1536]{1,0:T(8,128)(2,1)}, u32[]{:S(2)}, u32[]{:S(2)}) collective-permute-start(bf16[512,1536]{1,0:T(8,128)(2,1)S(1)} %collective-permute-done.15.refs_1_), channel_id=1, source_target_pairs={{0,1},{1,0},{2,3},{3,2},{4,5},{5,4},{6,7},{7,6},{8,9},{9,8},{10,11... | collective-permute-start | bytes 4718600 | tf_op jit(solution)/shard_map/ppermute | solution.py:686
  175.0 41.3 %collective-permute-start.19 = (bf16[512,1536]{1,0:T(8,128)(2,1)}, bf16[512,1536]{1,0:T(8,128)(2,1)}, u32[]{:S(2)}, u32[]{:S(2)}) collective-permute-start(bf16[512,1536]{1,0:T(8,128)(2,1)} %collective-permute-done.14.refs_1_), channel_id=1, source_target_pairs={{0,1},{1,0},{2,3},{3,2},{4,5},{5,4},{6,7},{7,6},{8,9},{9,8},{10,11... | collective-permute-start | bytes 4718600 | tf_op jit(solution)/shard_map/ppermute | solution.py:686
  175.5 40.8 %collective-permute-start.18 = (bf16[512,1536]{1,0:T(8,128)(2,1)}, bf16[512,1536]{1,0:T(8,128)(2,1)}, u32[]{:S(2)}, u32[]{:S(2)}) collective-permute-start(bf16[512,1536]{1,0:T(8,128)(2,1)} %refs_0_.2), channel_id=1, source_target_pairs={{0,1},{1,0},{2,3},{3,2},{4,5},{5,4},{6,7},{7,6},{8,9},{9,8},{10,11... | collective-permute-start | bytes 4718600 | tf_op jit(solution)/shard_map/ppermute | solution.py:686
  250.0 5.9 %collective-permute-start.20 = (bf16[1024,1536]{1,0:T(8,128)(2,1)}, bf16[1024,1536]{1,0:T(8,128)(2,1)S(1)}, u32[]{:S(2)}, u32[]{:S(2)}) collective-permute-start(bf16[1024,1536]{1,0:T(8,128)(2,1)} %get-tuple-element.119), channel_id=1, source_target_pairs={{0,1},{1,0},{2,3},{3,2},{4,5},{5,4},{6,7},{7,6},{8,9},{9,8},{10,11... | collective-permute-start | bytes 9437192 | tf_op jit(solution)/shard_map/ppermute | solution.py:686
  260.6 36.8 %collective-permute-start.21 = (bf16[512,1536]{1,0:T(8,128)(2,1)}, bf16[512,1536]{1,0:T(8,128)(2,1)}, u32[]{:S(2)}, u32[]{:S(2)}) collective-permute-start(bf16[512,1536]{1,0:T(8,128)(2,1)} %add_convert_fusion.3), channel_id=1, source_target_pairs={{0,8},{1,9},{2,10},{3,11},{4,12},{5,13},{6,14},{7,15},{8,0},{9,1},... | collective-permute-start | bytes 4718600 | tf_op jit(solution)/shard_map/ppermute | solution.py:686
  290.6 21.7 %collective-permute-start.22 = (bf16[1024,1536]{1,0:T(8,128)(2,1)}, bf16[1024,1536]{1,0:T(8,128)(2,1)}, u32[]{:S(2)}, u32[]{:S(2)}) collective-permute-start(bf16[1024,1536]{1,0:T(8,128)(2,1)} %get-tuple-element.123), channel_id=1, source_target_pairs={{0,1},{1,0},{2,3},{3,2},{4,5},{5,4},{6,7},{7,6},{8,9},{9,8},{10,11... | collective-permute-start | bytes 9437192 | tf_op jit(solution)/shard_map/ppermute | solution.py:686
  291.2 220.1 %reduce-scatter.5.cloned.1.call-start = ((), (), s32[]{:S(2)}) async-start(), calls=%async_computation.5 | async-start | bytes 3538944 | tf_op jit(solution)/shard_map/reduce_scatter | solution.py:1072
  315.4 38.4 %collective-permute-start.23 = (bf16[512,1536]{1,0:T(8,128)(2,1)}, bf16[512,1536]{1,0:T(8,128)(2,1)}, u32[]{:S(2)}, u32[]{:S(2)}) collective-permute-start(bf16[512,1536]{1,0:T(8,128)(2,1)} %add_convert_fusion.2), channel_id=1, source_target_pairs={{0,8},{1,9},{2,10},{3,11},{4,12},{5,13},{6,14},{7,15},{8,0},{9,1},... | collective-permute-start | bytes 4718600 | tf_op jit(solution)/shard_map/ppermute | solution.py:686
  366.5 8.1 %collective-permute-start.25 = (bf16[1536,1536]{1,0:T(8,128)(2,1)}, bf16[1536,1536]{1,0:T(8,128)(2,1)S(1)}, u32[]{:S(2)}, u32[]{:S(2)}) collective-permute-start(bf16[1536,1536]{1,0:T(8,128)(2,1)} %packed_slots.4), channel_id=1, source_target_pairs={{0,1},{1,0},{2,3},{3,2},{4,5},{5,4},{6,7},{7,6},{8,9},{9,8},{10,11... | collective-permute-start | bytes 14155784 | tf_op jit(solution)/shard_map/ppermute | solution.py:686
  366.5 5.9 %collective-permute-start.24 = (f32[32,128]{1,0:T(8,128)S(1)}, f32[32,128]{1,0:T(8,128)S(1)}, u32[]{:S(2)}, u32[]{:S(2)}) collective-permute-start(f32[32,128]{1,0:T(8,128)S(1)} %fusion.12), channel_id=1, source_target_pairs={{0,1},{1,0},{2,3},{3,2},{4,5},{5,4},{6,7},{7,6},{8,9},{9,8},{10,11... | collective-permute-start | bytes 49160 | tf_op jit(solution)/shard_map/ppermute | solution.py:686
  382.8 29.1 %collective-permute-start.27 = (bf16[768,1536]{1,0:T(8,128)(2,1)}, bf16[768,1536]{1,0:T(8,128)(2,1)S(1)}, u32[]{:S(2)}, u32[]{:S(2)}) collective-permute-start(bf16[768,1536]{1,0:T(8,128)(2,1)} %packed_slots.5), channel_id=1, source_target_pairs={{0,8},{1,17},{2,10},{3,19},{4,12},{5,21},{6,14},{7,23},{8,0},{9,25... | collective-permute-start | bytes 7077896 | tf_op jit(solution)/shard_map/ppermute | solution.py:686
  399.2 8.6 %collective-permute-start.26 = (f32[32,128]{1,0:T(8,128)S(1)}, f32[32,128]{1,0:T(8,128)S(1)}, u32[]{:S(2)}, u32[]{:S(2)}) collective-permute-start(f32[32,128]{1,0:T(8,128)S(1)} %add.281), channel_id=1, source_target_pairs={{0,2},{1,3},{2,0},{3,1},{4,6},{5,7},{6,4},{7,5},{8,10},{9,11},{10,... | collective-permute-start | bytes 49160 | tf_op jit(solution)/shard_map/ppermute | solution.py:686
  417.6 23.7 %collective-permute-start.29 = (bf16[384,1536]{1,0:T(8,128)(2,1)}, bf16[384,1536]{1,0:T(8,128)(2,1)S(1)}, u32[]{:S(2)}, u32[]{:S(2)}) collective-permute-start(bf16[384,1536]{1,0:T(8,128)(2,1)} %packed_slots.6), channel_id=1, source_target_pairs={{0,16},{1,9},{2,18},{3,11},{4,20},{5,13},{6,22},{7,15},{8,24},{9,1... | collective-permute-start | bytes 3538952 | tf_op jit(solution)/shard_map/ppermute | solution.py:686
  418.2 4.8 collective-permute-start.28
  447.3 12.0 %collective-permute-start.30 = (bf16[192,2048]{1,0:T(8,128)(2,1)S(1)}, bf16[192,2048]{1,0:T(8,128)(2,1)S(1)}, u32[]{:S(2)}, u32[]{:S(2)}) collective-permute-start(bf16[192,2048]{1,0:T(8,128)(2,1)S(1)} %copy-done.27), channel_id=1, source_target_pairs={{0,8},{1,17},{2,10},{3,19},{4,12},{5,21},{6,14},{7,23},{8,0},{9,25... | collective-permute-start | bytes 2359304 | tf_op jit(solution)/shard_map/ppermute | solution.py:686
  449.2 19.1 %collective-permute-start.31 = (bf16[96,1536]{1,0:T(8,128)(2,1)S(1)}, bf16[96,1536]{1,0:T(8,128)(2,1)S(1)}, u32[]{:S(2)}, u32[]{:S(2)}) collective-permute-start(bf16[96,1536]{1,0:T(8,128)(2,1)S(1)} %get-tuple-element.181), channel_id=1, source_target_pairs={{0,2},{1,3},{2,4},{3,5},{4,6},{5,7},{6,0},{7,1},{8,10},{9,11},{10,... | collective-permute-start | bytes 884744 | tf_op jit(solution)/shard_map/ppermute | solution.py:686
  450.7 20.7 %collective-permute-start.32 = (bf16[96,1536]{1,0:T(8,128)(2,1)S(1)}, bf16[96,1536]{1,0:T(8,128)(2,1)S(1)}, u32[]{:S(2)}, u32[]{:S(2)}) collective-permute-start(bf16[96,1536]{1,0:T(8,128)(2,1)S(1)} %get-tuple-element.180), channel_id=1, source_target_pairs={{0,4},{1,5},{2,6},{3,7},{4,0},{5,1},{6,2},{7,3},{8,12},{9,13},{10,... | collective-permute-start | bytes 884744 | tf_op jit(solution)/shard_map/ppermute | solution.py:686
  452.1 21.1 %collective-permute-start.33 = (bf16[96,1536]{1,0:T(8,128)(2,1)S(1)}, bf16[96,1536]{1,0:T(8,128)(2,1)S(1)}, u32[]{:S(2)}, u32[]{:S(2)}) collective-permute-start(bf16[96,1536]{1,0:T(8,128)(2,1)S(1)} %get-tuple-element.179), channel_id=1, source_target_pairs={{0,6},{1,7},{2,0},{3,1},{4,2},{5,3},{6,4},{7,5},{8,14},{9,15},{10,... | collective-permute-start | bytes 884744 | tf_op jit(solution)/shard_map/ppermute | solution.py:686
  473.4 9.8 %collective-permute-start.34 = (bf16[96,1536]{1,0:T(8,128)(2,1)S(1)}, bf16[96,1536]{1,0:T(8,128)(2,1)S(1)}, u32[]{:S(2)}, u32[]{:S(2)}) collective-permute-start(bf16[96,1536]{1,0:T(8,128)(2,1)S(1)} %add_convert_fusion.4), channel_id=1, source_target_pairs={{0,8},{1,17},{2,10},{3,19},{4,12},{5,21},{6,14},{7,23},{8,0},{9,25... | collective-permute-start | bytes 884744 | tf_op jit(solution)/shard_map/ppermute | solution.py:686
  473.6 16.9 %collective-permute-start.36 = (bf16[96,1536]{1,0:T(8,128)(2,1)S(1)}, bf16[96,1536]{1,0:T(8,128)(2,1)S(1)}, u32[]{:S(2)}, u32[]{:S(2)}) collective-permute-start(bf16[96,1536]{1,0:T(8,128)(2,1)S(1)} %add_convert_fusion.4), channel_id=1, source_target_pairs={{0,16},{1,9},{2,18},{3,11},{4,20},{5,13},{6,22},{7,15},{8,24},{9,1... | collective-permute-start | bytes 884744 | tf_op jit(solution)/shard_map/ppermute | solution.py:686
  483.2 7.3 %collective-permute-start.35 = (bf16[96,1536]{1,0:T(8,128)(2,1)S(1)}, bf16[96,1536]{1,0:T(8,128)(2,1)S(1)}, u32[]{:S(2)}, u32[]{:S(2)}) collective-permute-start(bf16[96,1536]{1,0:T(8,128)(2,1)S(1)} %collective-permute-done.34), channel_id=1, source_target_pairs={{0,16},{1,9},{2,18},{3,11},{4,20},{5,13},{6,22},{7,15},{8,24},{9,1... | collective-permute-start | bytes 884744 | tf_op jit(solution)/shard_map/ppermute | solution.py:686
  484.1 18.9 %collective-permute-start.39 = (bf16[192,2048]{1,0:T(8,128)(2,1)S(1)}, bf16[192,2048]{1,0:T(8,128)(2,1)S(1)}, u32[]{:S(2)}, u32[]{:S(2)}) collective-permute-start(bf16[192,2048]{1,0:T(8,128)(2,1)S(1)} %copy-done.27), channel_id=1, source_target_pairs={{0,16},{1,9},{2,18},{3,11},{4,20},{5,13},{6,22},{7,15},{8,24},{9,1... | collective-permute-start | bytes 2359304 | tf_op jit(solution)/shard_map/ppermute | solution.py:686
  488.5 10.2 %collective-permute-start.45 = (f32[32,128]{1,0:T(8,128)S(1)}, f32[32,128]{1,0:T(8,128)S(1)}, u32[]{:S(2)}, u32[]{:S(2)}) collective-permute-start(f32[32,128]{1,0:T(8,128)S(1)} %add.291), channel_id=1, source_target_pairs={{0,16},{1,17},{2,18},{3,19},{4,20},{5,21},{6,22},{7,23},{8,24},{9,... | collective-permute-start | bytes 49160 | tf_op jit(solution)/shard_map/ppermute | solution.py:686
  489.9 17.3 %collective-permute-start.38 = (bf16[192,2048]{1,0:T(8,128)(2,1)S(1)}, bf16[192,2048]{1,0:T(8,128)(2,1)}, u32[]{:S(2)}, u32[]{:S(2)}) collective-permute-start(bf16[192,2048]{1,0:T(8,128)(2,1)S(1)} %collective-permute-done.30), channel_id=1, source_target_pairs={{0,16},{1,9},{2,18},{3,11},{4,20},{5,13},{6,22},{7,15},{8,24},{9,1... | collective-permute-start | bytes 2359304 | tf_op jit(solution)/shard_map/ppermute | solution.py:686
  501.4 10.2 %collective-permute-start.37 = (bf16[192,1152]{1,0:T(8,128)(2,1)}, bf16[192,1152]{1,0:T(8,128)(2,1)}, u32[]{:S(2)}, u32[]{:S(2)}) collective-permute-start(bf16[192,1152]{1,0:T(8,128)(2,1)} %broadcast_select_fusion.5), channel_id=1, source_target_pairs={{0,1},{1,0},{2,3},{3,2},{4,5},{5,4},{6,7},{7,6},{8,9},{9,8},{10,11... | collective-permute-start | bytes 1327112 | tf_op jit(solution)/shard_map/ppermute | solution.py:686
  510.9 22.1 %collective-permute-start.40 = (bf16[384,2048]{1,0:T(8,128)(2,1)S(1)}, bf16[384,2048]{1,0:T(8,128)(2,1)}, u32[]{:S(2)}, u32[]{:S(2)}) collective-permute-start(bf16[384,2048]{1,0:T(8,128)(2,1)S(1)} %get-tuple-element.160), channel_id=1, source_target_pairs={{0,1},{1,0},{2,3},{3,2},{4,5},{5,4},{6,7},{7,6},{8,9},{9,8},{10,11... | collective-permute-start | bytes 4718600 | tf_op jit(solution)/shard_map/ppermute | solution.py:686
  511.3 11.6 %collective-permute-start.41 = (bf16[128,1536]{1,0:T(8,128)(2,1)}, bf16[128,1536]{1,0:T(8,128)(2,1)S(1)}, u32[]{:S(2)}, u32[]{:S(2)}) collective-permute-start(bf16[128,1536]{1,0:T(8,128)(2,1)} %reduce-scatter.5.cloned.1.call-done), channel_id=1, source_target_pairs={{0,8},{1,17},{2,10},{3,19},{4,12},{5,21},{6,14},{7,23},{8,0},{9,25... | collective-permute-start | bytes 1179656 | tf_op jit(solution)/shard_map/ppermute | solution.py:686
  512.9 12.7 %collective-permute-start.43 = (bf16[128,1536]{1,0:T(8,128)(2,1)S(1)}, bf16[128,1536]{1,0:T(8,128)(2,1)S(1)}, u32[]{:S(2)}, u32[]{:S(2)}) collective-permute-start(bf16[128,1536]{1,0:T(8,128)(2,1)S(1)} %copy-done.29), channel_id=1, source_target_pairs={{0,16},{1,9},{2,18},{3,11},{4,20},{5,13},{6,22},{7,15},{8,24},{9,1... | collective-permute-start | bytes 1179656 | tf_op jit(solution)/shard_map/ppermute | solution.py:686
  523.0 7.8 %collective-permute-start.42 = (bf16[128,1536]{1,0:T(8,128)(2,1)S(1)}, bf16[128,1536]{1,0:T(8,128)(2,1)S(1)}, u32[]{:S(2)}, u32[]{:S(2)}) collective-permute-start(bf16[128,1536]{1,0:T(8,128)(2,1)S(1)} %collective-permute-done.41), channel_id=1, source_target_pairs={{0,16},{1,9},{2,18},{3,11},{4,20},{5,13},{6,22},{7,15},{8,24},{9,1... | collective-permute-start | bytes 1179656 | tf_op jit(solution)/shard_map/ppermute | solution.py:686
  (38 other events, 275.8 us)
Sparse Core Ops, SparseCore 0:
  51.0 102.3 all-gather.2
  156.2 60.0 all-gather.4
  291.4 116.3 reduce-scatter.2
  411.2 81.2 reduce-scatter.4
where the time goes:
time: 550 us; the launch traced here: 545 us
  Pallas kernels  208 us (38%)
  waiting for transfers between devices  204 us (37%)
  other arithmetic  60.1 us (11%)
  starting transfers between devices  31.4 us (6%)
  local copies, waits for them, and re-layouts  22.2 us (4%)
  between operations  15.4 us (3%)
    ppermute x46, waiting for transfers between devices, move(): return lax.ppermute(value, AXES, pairs)  191 us
    pallas_call x5, Pallas kernels, product(): pl.pallas_call(functools.partial(product_kernel, pairs=len(lefts), across...  37.9 us
    ppermute x46, starting transfers between devices, move(): return lax.ppermute(value, AXES, pairs)  31 us
    pallas_call x4, Pallas kernels, packed_slots(): pl.pallas_call(packed_slot_kernel, grid_spec=pltpu.PrefetchScalarGridSpec...  22.9 us
    pallas_call x1, Pallas kernels, gated(): pl.pallas_call(functools.partial(gated_kernel, count=len(blocks)), grid=(...  22.9 us
    pallas_call x1, Pallas kernels, pair_back(): pl.pallas_call(pair_back_kernel, grid=(width // tile,), in_specs=[pl.Bloc...  19.3 us
    pallas_call x1, Pallas kernels, pair_grad(): pl.pallas_call(pair_grad_kernel, grid=(2 * steps,), in_specs=[pl.BlockSpe...  18.5 us
    pallas_call x1, Pallas kernels, run_backward(): pl.pallas_call(functools.partial(attention_backward, head_size=head_size)...  16.7 us
  transfers between devices with their start and end apart: 50, of which 28 were waited for; matrix products, arithmetic and copies ran while one was open for 12% of the time, Pallas kernels for 31%

commit v1 on v0

--- a/solution.py
+++ b/solution.py
@@ -370,7 +370,7 @@
         outs[0][...] = total.astype(outs[0].dtype)
 
 
-def product(lefts, rights, across=False, kind="low", most=256):
+def product(lefts, rights, across=False, kind="low", most=512):
     rows = lefts[0].shape[0]
     wide = rights[0].shape[0 if across else 1]
     tile = tile_of(wide, most)
@@ -401,12 +401,8 @@
 
 
 def column_slot_kernel(at_ref, left_ref, *refs, count, added):
-    left = left_ref[...]
-    depth = left.shape[1] // count
-    total = None
-    for number in range(count):
-        term = dot_nn(left[:, number * depth : (number + 1) * depth], refs[number][...])
-        total = term if total is None else total + term
+    right = jnp.concatenate([ref[...] for ref in refs[:count]], axis=0)
+    total = dot_nn(left_ref[...], right)
     for ref in refs[count : count + added]:
         total = total + ref[...].astype(jnp.float32)
     refs[-1][...] = total.astype(jnp.bfloat16)

time: 550 us -> 550 us (level)
  no operation moved by 1% of the time
where the time goes in v1:
time: 550 us; the launch traced here: 544 us
  Pallas kernels  206 us (37%)
  waiting for transfers between devices  202 us (37%)
  other arithmetic  60.1 us (11%)
  starting transfers between devices  33.8 us (6%)
  local copies, waits for them, and re-layouts  22.3 us (4%)
  between operations  15.4 us (3%)
    ppermute x46, waiting for transfers between devices, move(): return lax.ppermute(value, AXES, pairs)  187 us
    pallas_call x5, Pallas kernels, product(): pl.pallas_call(functools.partial(product_kernel, pairs=len(lefts), across...  36.4 us
    ppermute x46, starting transfers between devices, move(): return lax.ppermute(value, AXES, pairs)  33.4 us
    pallas_call x1, Pallas kernels, gated(): pl.pallas_call(functools.partial(gated_kernel, count=len(blocks)), grid=(...  22.9 us
    pallas_call x4, Pallas kernels, packed_slots(): pl.pallas_call(packed_slot_kernel, grid_spec=pltpu.PrefetchScalarGridSpec...  22.6 us
    pallas_call x1, Pallas kernels, pair_back(): pl.pallas_call(pair_back_kernel, grid=(width // tile,), in_specs=[pl.Bloc...  19.5 us
    pallas_call x1, Pallas kernels, pair_grad(): pl.pallas_call(pair_grad_kernel, grid=(2 * steps,), in_specs=[pl.BlockSpe...  18.5 us
    pallas_call x1, Pallas kernels, run_backward(): pl.pallas_call(functools.partial(attention_backward, head_size=head_size)...  16.7 us
  transfers between devices with their start and end apart: 50, of which 28 were waited for; matrix products, arithmetic and copies ran while one was open for 12% of the time, Pallas kernels for 31%

profile of v1, /device:TPU:10, one launch (start us, length us, event | category | flops | bytes accessed | tf_op | source)
XLA Modules:
  0.0 543.7 jit_solution(13040215436717580993)
XLA Ops:
  11.2 4.7 split.1
  21.2 4.4 collective-permute-done.1
  28.8 18.0 %collective-permute-done.5 = bf16[96,1536]{1,0:T(8,128)(2,1)S(1)} collective-permute-done((bf16[96,1536]{1,0:T(8,128)(2,1)S(1)}, bf16[96,1536]{1,0:T(8,128)(2,1)S(1)}, u32[]{:S(2)}, u32[]{:S(2)}) %collective-permute-start.5) | collective-permute-done | bytes 294944 | tf_op jit(solution)/shard_map/ppermute | solution.py:682
  58.5 15.1 %collective-permute-done.9.refs_4_ = bf16[288,1536]{1,0:T(8,128)(2,1)} collective-permute-done((bf16[288,1536]{1,0:T(8,128)(2,1)}, bf16[288,1536]{1,0:T(8,128)(2,1)}, u32[]{:S(2)}, u32[]{:S(2)}) %collective-permute-start.9) | collective-permute-done | bytes 884768 | tf_op jit(solution)/shard_map/ppermute | solution.py:682
  75.7 3.4 multiply_convert_fusion.1.x_ref.refs_0_
  79.1 3.9 turn.1
  83.8 9.5 %collective-permute-done.11.refs_6_ = bf16[288,1536]{1,0:T(8,128)(2,1)S(1)} collective-permute-done((bf16[288,1536]{1,0:T(8,128)(2,1)}, bf16[288,1536]{1,0:T(8,128)(2,1)S(1)}, u32[]{:S(2)}, u32[]{:S(2)}) %collective-permute-start.11) | collective-permute-done | bytes 884768 | tf_op jit(solution)/shard_map/ppermute | solution.py:682
  94.1 5.6 %place.2 = (bf16[1536,1152]{1,0:T(8,128)(2,1)}, bf16[384,1536]{1,0:T(8,128)(2,1)}) custom-call(s32[2,27]{1,0:T(2,128)} %pad_add_fusion.1.at_ref, bf16[192,1152]{1,0:T(8,128)(2,1)} %copy-done.13, bf16[192,1152]{1,0:T(8,128)(2,1)} %copy-done.24, bf16[96,1536]{1,0:T(8,128)(2,1)} %refs_2_.1, bf16[288,1536]{1,0:T(8,128)(2,1)} %copy-done.17, ...), custom_call_target="tpu_custom_call" | custom-call | flops 1207959552 | bytes 2359296 | tf_op jit(solution)/shard_map/place/pallas_call | solution.py:337
  102.7 6.0 %product.5 = bf16[512,1152]{1,0:T(8,128)(2,1)} custom-call(bf16[512,1536]{1,0:T(8,128)(2,1)} %multiply_convert_fusion.1.x_ref.refs_0_, bf16[1536,1152]{1,0:T(8,128)(2,1)} %get-tuple-element.95.refs_1_), custom_call_target="tpu_custom_call" | custom-call | flops 1811939328 | bytes 3538944 | tf_op jit(solution)/shard_map/product/pallas_call | solution.py:390
  108.9 6.1 %product.6 = bf16[512,1152]{1,0:T(8,128)(2,1)} custom-call(bf16[512,1536]{1,0:T(8,128)(2,1)} %multiply_convert_fusion.1.x_ref.refs_0_, bf16[1536,1152]{1,0:T(8,128)(2,1)} %collective-permute-done.12.refs_1_.refs_3_), custom_call_target="tpu_custom_call" | custom-call | flops 1811939328 | bytes 3538944 | tf_op jit(solution)/shard_map/product/pallas_call | solution.py:390
  118.1 10.5 %attend.1 = (bf16[512,768]{1,0:T(8,128)(2,1)}, bf16[768,512]{1,0:T(8,128)(2,1)}, f32[6,2,512]{2,1,0:T(2,128)}) custom-call(s32[1]{0:T(128)S(6)} %copy.58.valid_ref, f32[6,2,1024]{2,1,0:T(2,128)} %copy.38.bias_ref, bf16[2,512,1152]{2,1,0:T(8,128)(2,1)} %pad_maximum_fusion.q_ref.k_ref.v_ref, bf16[2,512,1152]{2,1,0:T(8,128)(2,1)} %pad_maximum_fusion.q_ref.k_ref.v_ref, ...), custom_call_target="tpu_custom_call" | custom-call | flops 3221225472 | bytes 6291456 | tf_op jit(solution)/shard_map/attend/pallas_call | solution.py:128
  129.6 3.9 place.3.refs_1_
  140.5 34.4 %collective-permute-done.15.refs_1_ = bf16[512,1536]{1,0:T(8,128)(2,1)S(1)} collective-permute-done((bf16[512,1536]{1,0:T(8,128)(2,1)S(1)}, bf16[512,1536]{1,0:T(8,128)(2,1)S(1)}, u32[]{:S(2)}, u32[]{:S(2)}) %collective-permute-start.15) | collective-permute-done | bytes 1572896 | tf_op jit(solution)/shard_map/ppermute | solution.py:682
  177.2 3.5 collective-permute-done.17.refs_3_
  180.7 22.9 %gated.1 = (bf16[2048,1024]{1,0:T(8,128)(2,1)}, bf16[1024,2048]{1,0:T(8,128)(2,1)}, bf16[2048,1024]{1,0:T(8,128)(2,1)}, bf16[2048,1024]{1,0:T(8,128)(2,1)}) custom-call(bf16[512,1536]{1,0:T(8,128)(2,1)} %copy-done.11, bf16[512,1536]{1,0:T(8,128)(2,1)} %copy-done.15, bf16[512,1536]{1,0:T(8,128)(2,1)} %copy-done.16, ...), custom_call_target="tpu_custom_call" | custom-call | flops 12884901888 | bytes 25165824 | tf_op jit(solution)/shard_map/gated/pallas_call | solution.py:549
  203.6 7.5 %turn_team.1.left_ref = bf16[1536,2048]{1,0:T(8,128)(2,1)} custom-call(bf16[512,1536]{1,0:T(8,128)(2,1)} %copy-done.11, bf16[512,1536]{1,0:T(8,128)(2,1)} %copy-done.15, bf16[512,1536]{1,0:T(8,128)(2,1)} %copy-done.16, bf16[512,1536]{1,0:T(8,128)(2,1)} %collective-permute-done.17.refs_3_), custom_call_target="tpu_custom_call" | custom-call | flops 1610612736 | bytes 3145728 | tf_op jit(solution)/shard_map/turn_team/pallas_call | solution.py:295
  211.2 5.1 all-gather.5.cloned.1.call-done.refs_4_.refs_1_
  216.3 14.4 %gated_back.1.pair_ref.right_ref = bf16[2,2048,1024]{2,1,0:T(8,128)(2,1)} custom-call(bf16[512,1536]{1,0:T(8,128)(2,1)} %refs_0_.2, bf16[512,1536]{1,0:T(8,128)(2,1)} %collective-permute-done.14.refs_1_, bf16[512,1536]{1,0:T(8,128)(2,1)} %collective-permute-done.18.refs_2_, bf16[512,1536]{1,0:T(8,128)(2,1)} %collective-permute-done.19.refs_3_, ...), custom_call_target="tpu_custom_call" | custom-call | flops 6442450944 | bytes 12582912 | tf_op jit(solution)/shard_map/gated_back/pallas_call | solution.py:581
  230.7 19.5 %pair_back.1 = (f32[512,1536]{1,0:T(8,128)}, f32[512,1536]{1,0:T(8,128)}, bf16[1024,1536]{1,0:T(8,128)(2,1)}) custom-call(bf16[2,2048,1024]{2,1,0:T(8,128)(2,1)} %gated_back.1.pair_ref.right_ref, bf16[1536,2048]{1,0:T(8,128)(2,1)} %all-gather.3.cloned.1.call-done.refs_4_.refs_5_.right_ref), custom_call_target="tpu_custom_call" | custom-call | flops 12884901888 | bytes 25165824 | tf_op jit(solution)/shard_map/pair_back/pallas_call | solution.py:633
  250.2 5.9 %collective-permute-done.20 = bf16[1024,1536]{1,0:T(8,128)(2,1)S(1)} collective-permute-done((bf16[1024,1536]{1,0:T(8,128)(2,1)}, bf16[1024,1536]{1,0:T(8,128)(2,1)S(1)}, u32[]{:S(2)}, u32[]{:S(2)}) %collective-permute-start.20) | collective-permute-done | bytes 3145760 | tf_op jit(solution)/shard_map/ppermute | solution.py:682
  256.1 4.7 add_convert_fusion.3
  261.4 18.5 %pair_grad.1 = bf16[1536,2048]{1,0:T(8,128)(2,1)} custom-call(bf16[1536,2048]{1,0:T(8,128)(2,1)} %turn_team.1.left_ref, bf16[2,2048,1024]{2,1,0:T(8,128)(2,1)} %gated_back.1.pair_ref.right_ref), custom_call_target="tpu_custom_call" | custom-call | flops 12884901888 | bytes 25165824 | tf_op jit(solution)/shard_map/pair_grad/pallas_call | solution.py:603
  279.9 10.9 %product.7 = (f32[512,1536]{1,0:T(8,128)}, f32[512,1536]{1,0:T(8,128)}, bf16[1024,1536]{1,0:T(8,128)(2,1)}) custom-call(bf16[2048,1024]{1,0:T(8,128)(2,1)} %get-tuple-element.122.refs_0_, bf16[1024,1536]{1,0:T(8,128)(2,1)} %all-gather.5.cloned.1.call-done.refs_4_.refs_1_), custom_call_target="tpu_custom_call" | custom-call | flops 6442450944 | bytes 12582912 | tf_op jit(solution)/shard_map/product/pallas_call | solution.py:390
  291.5 6.1 %collective-permute-done.21 = bf16[512,1536]{1,0:T(8,128)(2,1)} collective-permute-done((bf16[512,1536]{1,0:T(8,128)(2,1)}, bf16[512,1536]{1,0:T(8,128)(2,1)}, u32[]{:S(2)}, u32[]{:S(2)}) %collective-permute-start.21) | collective-permute-done | bytes 1572896 | tf_op jit(solution)/shard_map/ppermute | solution.py:682
  297.6 4.1 multiply_reduce_fusion.1
  301.8 5.4 fusion.20
  307.2 4.8 product.8.dctx_ref
  315.6 16.7 %attend_back.1 = (bf16[2,512,384]{2,1,0:T(8,128)(2,1)}, bf16[2,512,384]{2,1,0:T(8,128)(2,1)}, bf16[2,512,384]{2,1,0:T(8,128)(2,1)}, f32[6,2,1024]{2,1,0:T(2,128)}) custom-call(s32[1]{0:T(128)S(6)} %copy.58.valid_ref, f32[6,2,1024]{2,1,0:T(2,128)} %copy.38.bias_ref, bf16[2,512,1152]{2,1,0:T(8,128)(2,1)} %pad_maximum_fusion.q_ref.k_ref.v_ref, ...), custom_call_target="tpu_custom_call" | custom-call | flops 6442450944 | bytes 12582912 | tf_op jit(solution)/shard_map/attend_back/pallas_call | solution.py:162
  336.6 8.6 %product.9 = f32[512,1536]{1,0:T(8,128)} custom-call(bf16[512,1152]{1,0:T(8,128)(2,1)} %get-tuple-element.146.refs_0_.grad_ref, bf16[1536,1152]{1,0:T(8,128)(2,1)} %get-tuple-element.95.refs_1_, bf16[512,1152]{1,0:T(8,128)(2,1)} %get-tuple-element.138.refs_2_.grad_ref, bf16[1536,1152]{1,0:T(8,128)(2,1)} %collective-permute-done.12.refs_1_.refs_3_), custom_call_target="tpu_custom_call" | custom-call | flops 3623878656 | bytes 7077888 | tf_op jit(solution)/shard_map/product/pallas_call | solution.py:390
  348.2 4.0 add_convert_fusion.1
  352.5 4.9 add_convert_fusion
  357.5 7.7 %packed_slots.4 = bf16[1536,1536]{1,0:T(8,128)(2,1)} custom-call(s32[4]{0:T(128)} %constant.176.clone.row_ref, s32[4]{0:T(128)} %add_add_fusion.1.at_ref, bf16[1536,512]{1,0:T(8,128)(2,1)} %bitcast.89, bf16[512,1152]{1,0:T(8,128)(2,1)} %get-tuple-element.138.refs_2_.grad_ref, bf16[384,512]{1,0:T(8,128)(2,1)} %bitcast.97, ...), custom_call_target="tpu_custom_call" | custom-call | flops 2415919104 | bytes 4718592 | tf_op jit(solution)/shard_map/packed_slots/pallas_call | solution.py:475
  366.3 4.8 collective-permute-done.24
  375.5 5.6 %packed_slots.5 = bf16[768,1536]{1,0:T(8,128)(2,1)} custom-call(s32[2]{0:T(128)} %constant.177.clone.row_ref, s32[2]{0:T(128)} %pad_add_fusion.3.at_ref, bf16[1536,512]{1,0:T(8,128)(2,1)} %bitcast.90, bf16[512,1152]{1,0:T(8,128)(2,1)} %get-tuple-element.146.refs_0_.grad_ref, bf16[384,512]{1,0:T(8,128)(2,1)} %bitcast.93, ...), custom_call_target="tpu_custom_call" | custom-call | flops 1207959552 | bytes 2359296 | tf_op jit(solution)/shard_map/packed_slots/pallas_call | solution.py:475
  383.3 14.2 %column_slots.1 = bf16[1024,1536]{1,0:T(8,128)(2,1)} custom-call(s32[4]{0:T(128)} %iota.9.at_ref, bf16[1024,2048]{1,0:T(8,128)(2,1)} %get-tuple-element.142.left_ref, bf16[512,1536]{1,0:T(8,128)(2,1)} %refs_0_.2, bf16[512,1536]{1,0:T(8,128)(2,1)} %collective-permute-done.14.refs_1_, bf16[512,1536]{1,0:T(8,128)(2,1)} %collective-permute-done.18.refs_2_, ...), custom_call_target="tpu_custom_call" | custom-call | flops 6442450944 | bytes 12582912 | tf_op jit(solution)/shard_map/column_slots/pallas_call | solution.py:424
  398.3 10.0 %reduce-scatter.3.cloned.1.call-done = bf16[192,2048]{1,0:T(8,128)(2,1)} async-done(((bf16[1536,2048]{1,0:T(8,128)(2,1)}), bf16[192,2048]{1,0:T(8,128)(2,1)}) %reduce-scatter.3.cloned.1.call-update) | async-done | bytes 786448 | tf_op jit(solution)/shard_map/reduce_scatter | solution.py:985
  411.6 4.3 packed_slots.6
  417.7 4.1 collective-permute-done.28
  421.8 18.7 %collective-permute-done.29.refs_2_ = bf16[384,1536]{1,0:T(8,128)(2,1)S(1)} collective-permute-done((bf16[384,1536]{1,0:T(8,128)(2,1)}, bf16[384,1536]{1,0:T(8,128)(2,1)S(1)}, u32[]{:S(2)}, u32[]{:S(2)}) %collective-permute-start.29) | collective-permute-done | bytes 1179680 | tf_op jit(solution)/shard_map/ppermute | solution.py:682
  441.6 4.9 packed_slots.7
  453.1 5.4 collective-permute-done.30
  458.5 10.0 %collective-permute-done.31 = bf16[96,1536]{1,0:T(8,128)(2,1)S(1)} collective-permute-done((bf16[96,1536]{1,0:T(8,128)(2,1)S(1)}, bf16[96,1536]{1,0:T(8,128)(2,1)S(1)}, u32[]{:S(2)}, u32[]{:S(2)}) %collective-permute-start.31) | collective-permute-done | bytes 294944 | tf_op jit(solution)/shard_map/ppermute | solution.py:682
  475.4 8.0 %collective-permute-done.34 = bf16[96,1536]{1,0:T(8,128)(2,1)S(1)} collective-permute-done((bf16[96,1536]{1,0:T(8,128)(2,1)S(1)}, bf16[96,1536]{1,0:T(8,128)(2,1)S(1)}, u32[]{:S(2)}, u32[]{:S(2)}) %collective-permute-start.34) | collective-permute-done | bytes 294944 | tf_op jit(solution)/shard_map/ppermute | solution.py:682
  491.0 7.9 %collective-permute-done.45 = f32[32,128]{1,0:T(8,128)S(1)} collective-permute-done((f32[32,128]{1,0:T(8,128)S(1)}, f32[32,128]{1,0:T(8,128)S(1)}, u32[]{:S(2)}, u32[]{:S(2)}) %collective-permute-start.45) | collective-permute-done | bytes 16416 | tf_op jit(solution)/shard_map/ppermute | solution.py:682
  503.2 4.2 collective-permute-done.38
  513.9 8.0 %collective-permute-done.41 = bf16[128,1536]{1,0:T(8,128)(2,1)S(1)} collective-permute-done((bf16[128,1536]{1,0:T(8,128)(2,1)}, bf16[128,1536]{1,0:T(8,128)(2,1)S(1)}, u32[]{:S(2)}, u32[]{:S(2)}) %collective-permute-start.41) | collective-permute-done | bytes 393248 | tf_op jit(solution)/shard_map/ppermute | solution.py:682
  525.3 4.4 collective-permute-done.42
  531.9 5.0 join.1
  (252 shorter events, 107.8 us)
Async XLA Ops:
  7.2 173.5 %all-gather.3.cloned.1.call-start = ((), (), s32[]{:S(2)}) async-start(), calls=%async_computation.2 | async-start | bytes 7077888 | tf_op jit(solution)/shard_map/all_gather | solution.py:875
  10.6 5.4 collective-permute-start
  16.1 12.6 %collective-permute-start.4 = (bf16[96,1536]{1,0:T(8,128)(2,1)S(1)}, bf16[96,1536]{1,0:T(8,128)(2,1)S(1)}, u32[]{:S(2)}, u32[]{:S(2)}) collective-permute-start(bf16[96,1536]{1,0:T(8,128)(2,1)S(1)} %pad_maximum_fusion.8), channel_id=1, source_target_pairs={{0,2},{1,3},{2,4},{3,5},{4,6},{5,7},{6,0},{7,1},{8,10},{9,11},{10,... | collective-permute-start | bytes 884744 | tf_op jit(solution)/shard_map/ppermute | solution.py:682
  17.9 7.7 %collective-permute-start.1 = (bf16[8,128]{1,0:T(8,128)(2,1)S(1)}, bf16[8,128]{1,0:T(8,128)(2,1)S(1)}, u32[]{:S(2)}, u32[]{:S(2)}) collective-permute-start(bf16[8,128]{1,0:T(8,128)(2,1)S(1)} %fusion.19), channel_id=1, source_target_pairs={{0,2},{1,3},{2,4},{3,5},{4,6},{5,7},{6,0},{7,1},{8,10},{9,11},{10,... | collective-permute-start | bytes 6152 | tf_op jit(solution)/shard_map/ppermute | solution.py:682
  19.5 8.7 %collective-permute-start.2 = (bf16[8,128]{1,0:T(8,128)(2,1)S(1)}, bf16[8,128]{1,0:T(8,128)(2,1)S(1)}, u32[]{:S(2)}, u32[]{:S(2)}) collective-permute-start(bf16[8,128]{1,0:T(8,128)(2,1)S(1)} %fusion.19), channel_id=1, source_target_pairs={{0,4},{1,5},{2,6},{3,7},{4,0},{5,1},{6,2},{7,3},{8,12},{9,13},{10,... | collective-permute-start | bytes 6152 | tf_op jit(solution)/shard_map/ppermute | solution.py:682
  20.7 8.0 %collective-permute-start.3 = (bf16[8,128]{1,0:T(8,128)(2,1)S(1)}, bf16[8,128]{1,0:T(8,128)(2,1)S(1)}, u32[]{:S(2)}, u32[]{:S(2)}) collective-permute-start(bf16[8,128]{1,0:T(8,128)(2,1)S(1)} %fusion.19), channel_id=1, source_target_pairs={{0,6},{1,7},{2,0},{3,1},{4,2},{5,3},{6,4},{7,5},{8,14},{9,15},{10,... | collective-permute-start | bytes 6152 | tf_op jit(solution)/shard_map/ppermute | solution.py:682
  21.2 27.5 %collective-permute-start.7 = (bf16[192,2048]{1,0:T(8,128)(2,1)}, bf16[192,2048]{1,0:T(8,128)(2,1)}, u32[]{:S(2)}, u32[]{:S(2)}) collective-permute-start(bf16[192,2048]{1,0:T(8,128)(2,1)} %get-tuple-element.84), channel_id=1, source_target_pairs={{0,1},{1,0},{2,3},{3,2},{4,5},{5,4},{6,7},{7,6},{8,9},{9,8},{10,11... | collective-permute-start | bytes 2359304 | tf_op jit(solution)/shard_map/ppermute | solution.py:682
  25.6 21.2 %collective-permute-start.5 = (bf16[96,1536]{1,0:T(8,128)(2,1)S(1)}, bf16[96,1536]{1,0:T(8,128)(2,1)S(1)}, u32[]{:S(2)}, u32[]{:S(2)}) collective-permute-start(bf16[96,1536]{1,0:T(8,128)(2,1)S(1)} %pad_maximum_fusion.8), channel_id=1, source_target_pairs={{0,4},{1,5},{2,6},{3,7},{4,0},{5,1},{6,2},{7,3},{8,12},{9,13},{10,... | collective-permute-start | bytes 884744 | tf_op jit(solution)/shard_map/ppermute | solution.py:682
  28.2 19.5 %collective-permute-start.6 = (bf16[96,1536]{1,0:T(8,128)(2,1)S(1)}, bf16[96,1536]{1,0:T(8,128)(2,1)S(1)}, u32[]{:S(2)}, u32[]{:S(2)}) collective-permute-start(bf16[96,1536]{1,0:T(8,128)(2,1)S(1)} %pad_maximum_fusion.8), channel_id=1, source_target_pairs={{0,6},{1,7},{2,0},{3,1},{4,2},{5,3},{6,4},{7,5},{8,14},{9,15},{10,... | collective-permute-start | bytes 884744 | tf_op jit(solution)/shard_map/ppermute | solution.py:682
  50.9 165.3 %all-gather.5.cloned.1.call-start = ((), (), s32[]{:S(2)}) async-start(), calls=%async_computation.3 | async-start | bytes 3538944 | tf_op jit(solution)/shard_map/all_gather | solution.py:876
  53.5 20.1 %collective-permute-start.9 = (bf16[288,1536]{1,0:T(8,128)(2,1)}, bf16[288,1536]{1,0:T(8,128)(2,1)}, u32[]{:S(2)}, u32[]{:S(2)}) collective-permute-start(bf16[288,1536]{1,0:T(8,128)(2,1)} %copy-done.17), channel_id=1, source_target_pairs={{0,8},{1,17},{2,10},{3,19},{4,12},{5,21},{6,14},{7,23},{8,0},{9,25... | collective-permute-start | bytes 2654216 | tf_op jit(solution)/shard_map/ppermute | solution.py:682
  57.4 26.4 %collective-permute-start.10 = (bf16[288,1536]{1,0:T(8,128)(2,1)S(1)}, bf16[288,1536]{1,0:T(8,128)(2,1)S(1)}, u32[]{:S(2)}, u32[]{:S(2)}) collective-permute-start(bf16[288,1536]{1,0:T(8,128)(2,1)S(1)} %copy-done.18), channel_id=1, source_target_pairs={{0,16},{1,9},{2,18},{3,11},{4,20},{5,13},{6,22},{7,15},{8,24},{9,1... | collective-permute-start | bytes 2654216 | tf_op jit(solution)/shard_map/ppermute | solution.py:682
  73.6 19.6 %collective-permute-start.11 = (bf16[288,1536]{1,0:T(8,128)(2,1)}, bf16[288,1536]{1,0:T(8,128)(2,1)S(1)}, u32[]{:S(2)}, u32[]{:S(2)}) collective-permute-start(bf16[288,1536]{1,0:T(8,128)(2,1)} %collective-permute-done.9.refs_4_), channel_id=1, source_target_pairs={{0,16},{1,9},{2,18},{3,11},{4,20},{5,13},{6,22},{7,15},{8,24},{9,1... | collective-permute-start | bytes 2654216 | tf_op jit(solution)/shard_map/ppermute | solution.py:682
  99.7 9.2 %collective-permute-start.12 = (bf16[1536,1152]{1,0:T(8,128)(2,1)}, bf16[1536,1152]{1,0:T(8,128)(2,1)}, u32[]{:S(2)}, u32[]{:S(2)}) collective-permute-start(bf16[1536,1152]{1,0:T(8,128)(2,1)} %get-tuple-element.95.refs_1_), channel_id=1, source_target_pairs={{0,1},{1,0},{2,3},{3,2},{4,5},{5,4},{6,7},{7,6},{8,9},{9,8},{10,11... | collective-permute-start | bytes 10616840 | tf_op jit(solution)/shard_map/ppermute | solution.py:682
  101.8 37.1 %collective-permute-start.14 = (bf16[512,1536]{1,0:T(8,128)(2,1)}, bf16[512,1536]{1,0:T(8,128)(2,1)}, u32[]{:S(2)}, u32[]{:S(2)}) collective-permute-start(bf16[512,1536]{1,0:T(8,128)(2,1)} %refs_0_.2), channel_id=1, source_target_pairs={{0,8},{1,9},{2,10},{3,11},{4,12},{5,13},{6,14},{7,15},{8,0},{9,1},... | collective-permute-start | bytes 4718600 | tf_op jit(solution)/shard_map/ppermute | solution.py:682
  102.4 305.9 %reduce-scatter.3.cloned.1.call-start = ((), (), s32[]{:S(2)}) async-start(), calls=%async_computation.4 | async-start | bytes 7077888 | tf_op jit(solution)/shard_map/reduce_scatter | solution.py:985
  108.7 19.9 %collective-permute-start.13 = (bf16[384,1536]{1,0:T(8,128)(2,1)S(1)}, bf16[384,1536]{1,0:T(8,128)(2,1)S(1)}, u32[]{:S(2)}, u32[]{:S(2)}) collective-permute-start(bf16[384,1536]{1,0:T(8,128)(2,1)S(1)} %copy-done.21), channel_id=1, source_target_pairs={{0,1},{1,0},{2,3},{3,2},{4,5},{5,4},{6,7},{7,6},{8,9},{9,8},{10,11... | collective-permute-start | bytes 3538952 | tf_op jit(solution)/shard_map/ppermute | solution.py:682
  138.9 36.0 %collective-permute-start.15 = (bf16[512,1536]{1,0:T(8,128)(2,1)S(1)}, bf16[512,1536]{1,0:T(8,128)(2,1)S(1)}, u32[]{:S(2)}, u32[]{:S(2)}) collective-permute-start(bf16[512,1536]{1,0:T(8,128)(2,1)S(1)} %multiply_convert_fusion.refs_0_), channel_id=1, source_target_pairs={{0,8},{1,9},{2,10},{3,11},{4,12},{5,13},{6,14},{7,15},{8,0},{9,1},... | collective-permute-start | bytes 4718600 | tf_op jit(solution)/shard_map/ppermute | solution.py:682
  139.5 36.0 %collective-permute-start.16 = (bf16[512,1536]{1,0:T(8,128)(2,1)S(1)}, bf16[512,1536]{1,0:T(8,128)(2,1)S(1)}, u32[]{:S(2)}, u32[]{:S(2)}) collective-permute-start(bf16[512,1536]{1,0:T(8,128)(2,1)S(1)} %multiply_convert_fusion.refs_0_), channel_id=1, source_target_pairs={{0,1},{1,0},{2,3},{3,2},{4,5},{5,4},{6,7},{7,6},{8,9},{9,8},{10,11... | collective-permute-start | bytes 4718600 | tf_op jit(solution)/shard_map/ppermute | solution.py:682
  175.0 5.8 %collective-permute-start.17 = (bf16[512,1536]{1,0:T(8,128)(2,1)S(1)}, bf16[512,1536]{1,0:T(8,128)(2,1)}, u32[]{:S(2)}, u32[]{:S(2)}) collective-permute-start(bf16[512,1536]{1,0:T(8,128)(2,1)S(1)} %collective-permute-done.15.refs_1_), channel_id=1, source_target_pairs={{0,1},{1,0},{2,3},{3,2},{4,5},{5,4},{6,7},{7,6},{8,9},{9,8},{10,11... | collective-permute-start | bytes 4718600 | tf_op jit(solution)/shard_map/ppermute | solution.py:682
  175.0 41.3 %collective-permute-start.19 = (bf16[512,1536]{1,0:T(8,128)(2,1)}, bf16[512,1536]{1,0:T(8,128)(2,1)}, u32[]{:S(2)}, u32[]{:S(2)}) collective-permute-start(bf16[512,1536]{1,0:T(8,128)(2,1)} %collective-permute-done.14.refs_1_), channel_id=1, source_target_pairs={{0,1},{1,0},{2,3},{3,2},{4,5},{5,4},{6,7},{7,6},{8,9},{9,8},{10,11... | collective-permute-start | bytes 4718600 | tf_op jit(solution)/shard_map/ppermute | solution.py:682
  175.5 40.8 %collective-permute-start.18 = (bf16[512,1536]{1,0:T(8,128)(2,1)}, bf16[512,1536]{1,0:T(8,128)(2,1)}, u32[]{:S(2)}, u32[]{:S(2)}) collective-permute-start(bf16[512,1536]{1,0:T(8,128)(2,1)} %refs_0_.2), channel_id=1, source_target_pairs={{0,1},{1,0},{2,3},{3,2},{4,5},{5,4},{6,7},{7,6},{8,9},{9,8},{10,11... | collective-permute-start | bytes 4718600 | tf_op jit(solution)/shard_map/ppermute | solution.py:682
  250.2 5.9 %collective-permute-start.20 = (bf16[1024,1536]{1,0:T(8,128)(2,1)}, bf16[1024,1536]{1,0:T(8,128)(2,1)S(1)}, u32[]{:S(2)}, u32[]{:S(2)}) collective-permute-start(bf16[1024,1536]{1,0:T(8,128)(2,1)} %get-tuple-element.119), channel_id=1, source_target_pairs={{0,1},{1,0},{2,3},{3,2},{4,5},{5,4},{6,7},{7,6},{8,9},{9,8},{10,11... | collective-permute-start | bytes 9437192 | tf_op jit(solution)/shard_map/ppermute | solution.py:682
  260.8 36.8 %collective-permute-start.21 = (bf16[512,1536]{1,0:T(8,128)(2,1)}, bf16[512,1536]{1,0:T(8,128)(2,1)}, u32[]{:S(2)}, u32[]{:S(2)}) collective-permute-start(bf16[512,1536]{1,0:T(8,128)(2,1)} %add_convert_fusion.3), channel_id=1, source_target_pairs={{0,8},{1,9},{2,10},{3,11},{4,12},{5,13},{6,14},{7,15},{8,0},{9,1},... | collective-permute-start | bytes 4718600 | tf_op jit(solution)/shard_map/ppermute | solution.py:682
  290.8 21.2 %collective-permute-start.22 = (bf16[1024,1536]{1,0:T(8,128)(2,1)}, bf16[1024,1536]{1,0:T(8,128)(2,1)}, u32[]{:S(2)}, u32[]{:S(2)}) collective-permute-start(bf16[1024,1536]{1,0:T(8,128)(2,1)} %get-tuple-element.123), channel_id=1, source_target_pairs={{0,1},{1,0},{2,3},{3,2},{4,5},{5,4},{6,7},{7,6},{8,9},{9,8},{10,11... | collective-permute-start | bytes 9437192 | tf_op jit(solution)/shard_map/ppermute | solution.py:682
  291.4 219.7 %reduce-scatter.5.cloned.1.call-start = ((), (), s32[]{:S(2)}) async-start(), calls=%async_computation.5 | async-start | bytes 3538944 | tf_op jit(solution)/shard_map/reduce_scatter | solution.py:1068
  315.0 37.5 %collective-permute-start.23 = (bf16[512,1536]{1,0:T(8,128)(2,1)}, bf16[512,1536]{1,0:T(8,128)(2,1)}, u32[]{:S(2)}, u32[]{:S(2)}) collective-permute-start(bf16[512,1536]{1,0:T(8,128)(2,1)} %add_convert_fusion.2), channel_id=1, source_target_pairs={{0,8},{1,9},{2,10},{3,11},{4,12},{5,13},{6,14},{7,15},{8,0},{9,1},... | collective-permute-start | bytes 4718600 | tf_op jit(solution)/shard_map/ppermute | solution.py:682
  365.2 8.1 %collective-permute-start.25 = (bf16[1536,1536]{1,0:T(8,128)(2,1)}, bf16[1536,1536]{1,0:T(8,128)(2,1)S(1)}, u32[]{:S(2)}, u32[]{:S(2)}) collective-permute-start(bf16[1536,1536]{1,0:T(8,128)(2,1)} %packed_slots.4), channel_id=1, source_target_pairs={{0,1},{1,0},{2,3},{3,2},{4,5},{5,4},{6,7},{7,6},{8,9},{9,8},{10,11... | collective-permute-start | bytes 14155784 | tf_op jit(solution)/shard_map/ppermute | solution.py:682
  365.2 5.9 %collective-permute-start.24 = (f32[32,128]{1,0:T(8,128)S(1)}, f32[32,128]{1,0:T(8,128)S(1)}, u32[]{:S(2)}, u32[]{:S(2)}) collective-permute-start(f32[32,128]{1,0:T(8,128)S(1)} %fusion.12), channel_id=1, source_target_pairs={{0,1},{1,0},{2,3},{3,2},{4,5},{5,4},{6,7},{7,6},{8,9},{9,8},{10,11... | collective-permute-start | bytes 49160 | tf_op jit(solution)/shard_map/ppermute | solution.py:682
  381.1 29.1 %collective-permute-start.27 = (bf16[768,1536]{1,0:T(8,128)(2,1)}, bf16[768,1536]{1,0:T(8,128)(2,1)S(1)}, u32[]{:S(2)}, u32[]{:S(2)}) collective-permute-start(bf16[768,1536]{1,0:T(8,128)(2,1)} %packed_slots.5), channel_id=1, source_target_pairs={{0,8},{1,17},{2,10},{3,19},{4,12},{5,21},{6,14},{7,23},{8,0},{9,25... | collective-permute-start | bytes 7077896 | tf_op jit(solution)/shard_map/ppermute | solution.py:682
  397.5 10.7 %collective-permute-start.26 = (f32[32,128]{1,0:T(8,128)S(1)}, f32[32,128]{1,0:T(8,128)S(1)}, u32[]{:S(2)}, u32[]{:S(2)}) collective-permute-start(f32[32,128]{1,0:T(8,128)S(1)} %add.281), channel_id=1, source_target_pairs={{0,2},{1,3},{2,0},{3,1},{4,6},{5,7},{6,4},{7,5},{8,10},{9,11},{10,... | collective-permute-start | bytes 49160 | tf_op jit(solution)/shard_map/ppermute | solution.py:682
  415.9 24.6 %collective-permute-start.29 = (bf16[384,1536]{1,0:T(8,128)(2,1)}, bf16[384,1536]{1,0:T(8,128)(2,1)S(1)}, u32[]{:S(2)}, u32[]{:S(2)}) collective-permute-start(bf16[384,1536]{1,0:T(8,128)(2,1)} %packed_slots.6), channel_id=1, source_target_pairs={{0,16},{1,9},{2,18},{3,11},{4,20},{5,13},{6,22},{7,15},{8,24},{9,1... | collective-permute-start | bytes 3538952 | tf_op jit(solution)/shard_map/ppermute | solution.py:682
  416.9 4.9 collective-permute-start.28
  446.5 12.0 %collective-permute-start.30 = (bf16[192,2048]{1,0:T(8,128)(2,1)S(1)}, bf16[192,2048]{1,0:T(8,128)(2,1)S(1)}, u32[]{:S(2)}, u32[]{:S(2)}) collective-permute-start(bf16[192,2048]{1,0:T(8,128)(2,1)S(1)} %copy-done.27), channel_id=1, source_target_pairs={{0,8},{1,17},{2,10},{3,19},{4,12},{5,21},{6,14},{7,23},{8,0},{9,25... | collective-permute-start | bytes 2359304 | tf_op jit(solution)/shard_map/ppermute | solution.py:682
  449.3 19.2 %collective-permute-start.31 = (bf16[96,1536]{1,0:T(8,128)(2,1)S(1)}, bf16[96,1536]{1,0:T(8,128)(2,1)S(1)}, u32[]{:S(2)}, u32[]{:S(2)}) collective-permute-start(bf16[96,1536]{1,0:T(8,128)(2,1)S(1)} %get-tuple-element.181), channel_id=1, source_target_pairs={{0,2},{1,3},{2,4},{3,5},{4,6},{5,7},{6,0},{7,1},{8,10},{9,11},{10,... | collective-permute-start | bytes 884744 | tf_op jit(solution)/shard_map/ppermute | solution.py:682
  450.9 20.8 %collective-permute-start.32 = (bf16[96,1536]{1,0:T(8,128)(2,1)S(1)}, bf16[96,1536]{1,0:T(8,128)(2,1)S(1)}, u32[]{:S(2)}, u32[]{:S(2)}) collective-permute-start(bf16[96,1536]{1,0:T(8,128)(2,1)S(1)} %get-tuple-element.180), channel_id=1, source_target_pairs={{0,4},{1,5},{2,6},{3,7},{4,0},{5,1},{6,2},{7,3},{8,12},{9,13},{10,... | collective-permute-start | bytes 884744 | tf_op jit(solution)/shard_map/ppermute | solution.py:682
  452.3 21.1 %collective-permute-start.33 = (bf16[96,1536]{1,0:T(8,128)(2,1)S(1)}, bf16[96,1536]{1,0:T(8,128)(2,1)S(1)}, u32[]{:S(2)}, u32[]{:S(2)}) collective-permute-start(bf16[96,1536]{1,0:T(8,128)(2,1)S(1)} %get-tuple-element.179), channel_id=1, source_target_pairs={{0,6},{1,7},{2,0},{3,1},{4,2},{5,3},{6,4},{7,5},{8,14},{9,15},{10,... | collective-permute-start | bytes 884744 | tf_op jit(solution)/shard_map/ppermute | solution.py:682
  473.5 9.8 %collective-permute-start.34 = (bf16[96,1536]{1,0:T(8,128)(2,1)S(1)}, bf16[96,1536]{1,0:T(8,128)(2,1)S(1)}, u32[]{:S(2)}, u32[]{:S(2)}) collective-permute-start(bf16[96,1536]{1,0:T(8,128)(2,1)S(1)} %add_convert_fusion.4), channel_id=1, source_target_pairs={{0,8},{1,17},{2,10},{3,19},{4,12},{5,21},{6,14},{7,23},{8,0},{9,25... | collective-permute-start | bytes 884744 | tf_op jit(solution)/shard_map/ppermute | solution.py:682
  474.2 16.5 %collective-permute-start.36 = (bf16[96,1536]{1,0:T(8,128)(2,1)S(1)}, bf16[96,1536]{1,0:T(8,128)(2,1)S(1)}, u32[]{:S(2)}, u32[]{:S(2)}) collective-permute-start(bf16[96,1536]{1,0:T(8,128)(2,1)S(1)} %add_convert_fusion.4), channel_id=1, source_target_pairs={{0,16},{1,9},{2,18},{3,11},{4,20},{5,13},{6,22},{7,15},{8,24},{9,1... | collective-permute-start | bytes 884744 | tf_op jit(solution)/shard_map/ppermute | solution.py:682
  483.4 7.3 %collective-permute-start.35 = (bf16[96,1536]{1,0:T(8,128)(2,1)S(1)}, bf16[96,1536]{1,0:T(8,128)(2,1)S(1)}, u32[]{:S(2)}, u32[]{:S(2)}) collective-permute-start(bf16[96,1536]{1,0:T(8,128)(2,1)S(1)} %collective-permute-done.34), channel_id=1, source_target_pairs={{0,16},{1,9},{2,18},{3,11},{4,20},{5,13},{6,22},{7,15},{8,24},{9,1... | collective-permute-start | bytes 884744 | tf_op jit(solution)/shard_map/ppermute | solution.py:682
  484.7 18.5 %collective-permute-start.39 = (bf16[192,2048]{1,0:T(8,128)(2,1)S(1)}, bf16[192,2048]{1,0:T(8,128)(2,1)S(1)}, u32[]{:S(2)}, u32[]{:S(2)}) collective-permute-start(bf16[192,2048]{1,0:T(8,128)(2,1)S(1)} %copy-done.27), channel_id=1, source_target_pairs={{0,16},{1,9},{2,18},{3,11},{4,20},{5,13},{6,22},{7,15},{8,24},{9,1... | collective-permute-start | bytes 2359304 | tf_op jit(solution)/shard_map/ppermute | solution.py:682
  488.7 10.2 %collective-permute-start.45 = (f32[32,128]{1,0:T(8,128)S(1)}, f32[32,128]{1,0:T(8,128)S(1)}, u32[]{:S(2)}, u32[]{:S(2)}) collective-permute-start(f32[32,128]{1,0:T(8,128)S(1)} %add.291), channel_id=1, source_target_pairs={{0,16},{1,17},{2,18},{3,19},{4,20},{5,21},{6,22},{7,23},{8,24},{9,... | collective-permute-start | bytes 49160 | tf_op jit(solution)/shard_map/ppermute | solution.py:682
  490.2 17.2 %collective-permute-start.38 = (bf16[192,2048]{1,0:T(8,128)(2,1)S(1)}, bf16[192,2048]{1,0:T(8,128)(2,1)}, u32[]{:S(2)}, u32[]{:S(2)}) collective-permute-start(bf16[192,2048]{1,0:T(8,128)(2,1)S(1)} %collective-permute-done.30), channel_id=1, source_target_pairs={{0,16},{1,9},{2,18},{3,11},{4,20},{5,13},{6,22},{7,15},{8,24},{9,1... | collective-permute-start | bytes 2359304 | tf_op jit(solution)/shard_map/ppermute | solution.py:682
  501.7 10.0 %collective-permute-start.37 = (bf16[192,1152]{1,0:T(8,128)(2,1)}, bf16[192,1152]{1,0:T(8,128)(2,1)}, u32[]{:S(2)}, u32[]{:S(2)}) collective-permute-start(bf16[192,1152]{1,0:T(8,128)(2,1)} %broadcast_select_fusion.5), channel_id=1, source_target_pairs={{0,1},{1,0},{2,3},{3,2},{4,5},{5,4},{6,7},{7,6},{8,9},{9,8},{10,11... | collective-permute-start | bytes 1327112 | tf_op jit(solution)/shard_map/ppermute | solution.py:682
  511.1 20.8 %collective-permute-start.40 = (bf16[384,2048]{1,0:T(8,128)(2,1)S(1)}, bf16[384,2048]{1,0:T(8,128)(2,1)}, u32[]{:S(2)}, u32[]{:S(2)}) collective-permute-start(bf16[384,2048]{1,0:T(8,128)(2,1)S(1)} %get-tuple-element.160), channel_id=1, source_target_pairs={{0,1},{1,0},{2,3},{3,2},{4,5},{5,4},{6,7},{7,6},{8,9},{9,8},{10,11... | collective-permute-start | bytes 4718600 | tf_op jit(solution)/shard_map/ppermute | solution.py:682
  511.1 10.8 %collective-permute-start.41 = (bf16[128,1536]{1,0:T(8,128)(2,1)}, bf16[128,1536]{1,0:T(8,128)(2,1)S(1)}, u32[]{:S(2)}, u32[]{:S(2)}) collective-permute-start(bf16[128,1536]{1,0:T(8,128)(2,1)} %reduce-scatter.5.cloned.1.call-done), channel_id=1, source_target_pairs={{0,8},{1,17},{2,10},{3,19},{4,12},{5,21},{6,14},{7,23},{8,0},{9,25... | collective-permute-start | bytes 1179656 | tf_op jit(solution)/shard_map/ppermute | solution.py:682
  512.9 12.4 %collective-permute-start.43 = (bf16[128,1536]{1,0:T(8,128)(2,1)S(1)}, bf16[128,1536]{1,0:T(8,128)(2,1)S(1)}, u32[]{:S(2)}, u32[]{:S(2)}) collective-permute-start(bf16[128,1536]{1,0:T(8,128)(2,1)S(1)} %copy-done.29), channel_id=1, source_target_pairs={{0,16},{1,9},{2,18},{3,11},{4,20},{5,13},{6,22},{7,15},{8,24},{9,1... | collective-permute-start | bytes 1179656 | tf_op jit(solution)/shard_map/ppermute | solution.py:682
  521.9 7.8 %collective-permute-start.42 = (bf16[128,1536]{1,0:T(8,128)(2,1)S(1)}, bf16[128,1536]{1,0:T(8,128)(2,1)S(1)}, u32[]{:S(2)}, u32[]{:S(2)}) collective-permute-start(bf16[128,1536]{1,0:T(8,128)(2,1)S(1)} %collective-permute-done.41), channel_id=1, source_target_pairs={{0,16},{1,9},{2,18},{3,11},{4,20},{5,13},{6,22},{7,15},{8,24},{9,1... | collective-permute-start | bytes 1179656 | tf_op jit(solution)/shard_map/ppermute | solution.py:682
  (38 other events, 275.0 us)
Sparse Core Ops, SparseCore 0:
  51.0 102.3 all-gather.2
  156.2 60.0 all-gather.4
  291.6 116.6 reduce-scatter.2
  411.7 83.5 reduce-scatter.4
